TPU v7x, 32 devices: a whole 2x2x4 slice. The times are simulated.
32 devices in a mesh: row: 16 (over z, y, x), col: 2 (over core).
Axes of the slice: x: 2, y: 2, z: 4, core: 2. Of those that a mesh axis runs over, the one named last changes fastest.
Arguments:
- c_left: float32 [16, 2, 2048, 256], P('row', 'col'), may hold values from -6 to 6
- c_right: float32 [16, 2, 2048, 256], P('row', 'col'), may hold values from -6 to 6
- c_rank: int32 [16, 2], P('row', 'col'), may hold values from 32 to 256, as said below
- a_left: bfloat16 [16, 2, 2048, 256], P('row', None, 'col'), may hold values from -6 to 6
- a_right: bfloat16 [16, 2, 2048, 256], P('row', None, 'col'), may hold values from -0.125 to 0.125
- a_rank: int32 [16, 2], P('row'), may hold values from 32 to 256, as said below
- a_pattern: int32 [16, 2], P('row'), may hold values 0 or 1
- b_left: bfloat16 [2, 2, 2048, 256], P(None, 'col', 'row'), may hold values from -6 to 6
- b_right: bfloat16 [2, 2, 2048, 256], P(None, 'col', 'row'), may hold values from -0.375 to 0.375
- b_rank: int32 [2, 2], P(None, 'col'), may hold values from 32 to 256, as said below
- b_pattern: int32 [2, 2], P(None, 'col'), may hold values 0 or 1
- probe: bfloat16 [2, 2048, 256], replicated, may hold values from -6 to 6
- target: int32 [16, 2, 2], P('row', 'col'), may hold values from 16 to 240, as said below
Outputs:
- out_left: float32 [16, 2, 2048, 256], P('row', 'col')
- out_right: float32 [16, 2, 2048, 256], P('row', 'col')
Inputs may be any that keep to these rules, and one draw needn't show every extreme that they name: `c_rank`: every rank lies from 32 to 256; both ends are taken by some tile. `a_rank`: every rank lies from 32 to 256; both ends are taken by some tile. `b_rank`: every rank lies from 32 to 256; both ends are taken by some tile. With g(r) = max(8, r // 16): target[i, j, 0] <= c_rank[i, j] - g(c_rank[i, j]) and target[i, j, k] <= target[i, j, k - 1] - g(target[i, j, k - 1]); both ends are taken by some tile.
All inputs are finite; a program needn't handle non-finite values. No bound on the sum of `a_pattern` or of `b_pattern` on one device may be relied on, other than what follows from the above.
Results may differ from a plain program's by a relative error of at most 0.0009.
Values may be sent and summed in bfloat16 or wider, within the bound.
No kernel may reach another device: no remote copies, remote signals or barrier semaphores. Data moves between devices by JAX's collectives and lax.ppermute only.
A program may use at most 128 MiB of HBM per device.

v0:
```python
import functools
import math

import jax
import jax.numpy as jnp
from jax import lax
from jax.experimental import pallas as pl
from jax.experimental.pallas import tpu as pltpu
from jax.sharding import PartitionSpec as P

F32 = jnp.float32
BF16 = jnp.bfloat16
ANY = pl.ANY
VMEM = pltpu.VMEM
SMEM = pltpu.SMEM
PANEL = 64
CHUNK = 256


def exchange(x, axis, size, bit):
    return lax.ppermute(x, axis, [(r, r ^ bit) for r in range(size)])


def spread(x, axis, size, bits):
    masks = [0]
    for bit in bits:
        masks += [mask ^ bit for mask in masks]
    masks = sorted(masks, reverse=True)[:-1]
    return [x] + [exchange(x, axis, size, mask) for mask in masks], [0] + masks


def forwarded(x, axis, size, bits):
    blocks, masks = [x], [0]
    for bit in bits:
        blocks += [exchange(block, axis, size, bit) for block in blocks]
        masks += [mask ^ bit for mask in masks]
    return blocks, masks


def after(x, *before):
    return lax.optimization_barrier((x, *before))[0]


def bits_of(size):
    bits = []
    bit = size // 2
    while bit >= 1:
        bits.append(bit)
        bit //= 2
    return bits


def split2(x):
    high = x.astype(BF16)
    return high, (x - high.astype(F32)).astype(BF16)


def mm(a, b):
    return lax.dot_general(a, b, (((1,), (0,)), ((), ())), preferred_element_type=F32)


def mm_at(a, b):
    return lax.dot_general(a, b, (((0,), (0,)), ((), ())), preferred_element_type=F32)


def mm_bt(a, b):
    return lax.dot_general(a, b, (((1,), (1,)), ((), ())), preferred_element_type=F32)


def close(a, b):
    a_h, a_m = split2(a)
    b_h, b_m = split2(b)
    return mm(jnp.concatenate([a_h, a_m, a_h], 1), jnp.concatenate([b_h, b_h, b_m], 0))


def close_at(a, b):
    a_h, a_m = split2(a)
    b_h, b_m = split2(b)
    return mm_at(jnp.concatenate([a_h, a_m, a_h], 0), jnp.concatenate([b_h, b_h, b_m], 0))


def close_bt(a, b):
    a_h, a_m = split2(a)
    b_h, b_m = split2(b)
    return mm_bt(jnp.concatenate([a_h, a_m, a_h], 1), jnp.concatenate([b_h, b_h, b_m], 1))


def exact(a, b):
    return lax.dot_general(
        a, b, (((1,), (0,)), ((), ())), precision=lax.Precision.HIGHEST, preferred_element_type=F32
    )


def exact_at(a, b):
    return lax.dot_general(
        a, b, (((0,), (0,)), ((), ())), precision=lax.Precision.HIGHEST, preferred_element_type=F32
    )


def lanes_below(count, rows, width):
    return (lax.broadcasted_iota(jnp.int32, (rows, width), 1) < count).astype(F32)


def rows_below(count, rows, width):
    return (lax.broadcasted_iota(jnp.int32, (rows, width), 0) < count).astype(F32)


def place(srcs, masks, index, dst, sems, first):
    copies = []
    for src, owners in zip(srcs, masks):
        for at, mask in enumerate(owners):
            block = src.at[at]
            rows = block.shape[0]
            start = pl.multiple_of((index ^ mask) * rows, 16)
            copies.append(
                pltpu.make_async_copy(block, dst.at[pl.ds(start, rows), :], sems.at[first + len(copies)])
            )
    return copies


def lane_of(x, at):
    return jnp.broadcast_to(x[:, at : at + 1], (8, 128))


def row_of(x, at):
    return jnp.broadcast_to(x[at : at + 1, :], (8, x.shape[1]))


def factor_panel(rows, first, width, between):
    count = len(rows)
    lane = lax.broadcasted_iota(jnp.int32, (8, width), 1)
    sub_wide = lax.broadcasted_iota(jnp.int32, (8, width), 0)
    sub = lax.broadcasted_iota(jnp.int32, (8, 128), 0)
    wide = lambda x: jnp.concatenate([x] * (width // 128), 1)
    for s in range(count):
        c0 = first + 8 * s
        col = {}
        for l in range(8):
            for q in range(s, count):
                col[l, q] = lane_of(rows[q], c0 + l)
        inside = (lane >= c0) & (lane < c0 + 8)
        unit = jnp.where(lane == c0 + sub_wide, 1.0, 0.0)
        for q in range(s, count):
            rows[q] = jnp.where(inside, unit if q == s else 0.0, rows[q])
        pivots = jnp.ones((8, 128), F32)
        for l in range(8):
            d = row_of(col[l, s], l)
            inverse = 1.0 / d
            pivots = jnp.where(sub == l, d, pivots)
            mult = {}
            for q in range(s, count):
                mult[q] = col[l, q] * inverse
                if q == s:
                    mult[q] = jnp.where(sub > l, mult[q], 0.0)
            for l2 in range(l + 1, 8):
                e = row_of(col[l, s], l2)
                for q in range(s, count):
                    col[l2, q] = col[l2, q] - mult[q] * e
            pivot_row = row_of(rows[s], l)
            for q in range(s, count):
                rows[q] = rows[q] - wide(mult[q]) * pivot_row
        rows[s] = rows[s] * wide(lax.rsqrt(pivots))
        between(c0 // 8)
    return rows


def inverse_factor(work, beside=()):
    n = work.shape[0]
    beside = list(beside)
    slots = n // PANEL
    for p in range(slots):
        a = p * PANEL
        b = a + PANEL
        rows = [work[a + 8 * i : a + 8 * i + 8, :] for i in range(PANEL // 8)]
        rows = factor_panel(rows, a, n, functools.partial(some_of, beside, n // 8))
        for i in range(PANEL // 8):
            work[a + 8 * i : a + 8 * i + 8, :] = rows[i]
        if b < n:
            full = jnp.concatenate(rows, 0)
            lane = lax.broadcasted_iota(jnp.int32, (PANEL, n), 1)
            row = lax.broadcasted_iota(jnp.int32, (PANEL, n), 0)
            kept = jnp.where((lane > a + row) & (lane < b), 0.0, full)
            base = b // 128 * 128
            update = exact_at(full[:, base:], kept)[b - base :]
            lane = lax.broadcasted_iota(jnp.int32, (n - b, n), 1)
            rest = jnp.where((lane >= a) & (lane < b), 0.0, work[b:, :])
            work[b:, :] = rest - update
    while beside:
        beside.pop(0)()
    row = lax.broadcasted_iota(jnp.int32, (n, n), 0)
    lane = lax.broadcasted_iota(jnp.int32, (n, n), 1)
    work[...] = jnp.where(lane <= row, work[...], 0.0)


def some_of(beside, slabs, slab):
    for _ in range(-(-len(beside) // (slabs - slab))):
        beside.pop(0)()


def unit_beyond(count, width):
    row = lax.broadcasted_iota(jnp.int32, (width, width), 0)
    lane = lax.broadcasted_iota(jnp.int32, (width, width), 1)
    return jnp.where((row == lane) & (row >= count), 1.0, 0.0)


def probe_kernel(steps, right, probe, out, right_v, probe_v, sems):
    tile, width = right_v.shape
    copies = [pltpu.make_async_copy(right, right_v, sems.at[0])]
    for k in range(steps):
        here = probe_v.at[:, pl.ds(k * width, width)]
        copies.append(pltpu.make_async_copy(probe.at[k], here, sems.at[1 + k]))
    for copy in copies:
        copy.start()
    for copy in copies:
        copy.wait()
    high, mid = split2(right_v[...])
    both = probe_v[...]
    total = mm_at(high, both) + mm_at(mid, both)
    for k in range(steps):
        out[k] = total[:, k * width : (k + 1) * width]


def cross_kernel(masks_a, steps, scal, left, *refs):
    al, (out, left_v, parts_v, sems) = refs[: len(masks_a)], refs[len(masks_a) :]
    tile, width = left_v.shape
    copy_left = pltpu.make_async_copy(left, left_v, sems.at[0])
    copies = []
    for k in range(steps):
        here = parts_v.at[:, pl.ds((2 + k) * width, width)]
        copies += place([r.at[:, k] for r in al], masks_a, scal[1 + 4 * steps], here, sems, 1 + len(copies))
    copy_left.start()
    for copy in copies:
        copy.start()
    copy_left.wait()
    high, mid = split2(left_v[...])
    parts_v[:, :width] = high
    parts_v[:, width : 2 * width] = mid
    for copy in copies:
        copy.wait()
    x = mm_at(parts_v[:, :width], parts_v[...])
    y = mm_at(parts_v[:, width : 2 * width], parts_v[:, width:])
    hm = x[:, width : 2 * width]
    out[:width, :width] = x[:, :width] + hm + hm.T + y[:, :width]
    la = x[:, 2 * width :] + y[:, width:]
    out[:width, width:] = la
    out[width:, :width] = la.T
    out[width:, width:] = mm_at(parts_v[:, 2 * width :], parts_v[:, 2 * width :])


def order_kernel(masks_a, masks_b, steps, scal, probe, *refs):
    ar, (ar_out, probe_out, ar_v, probe_v, sems) = refs[: len(masks_a)], refs[len(masks_a) :]
    col_at, row_at = scal[1 + 4 * steps], scal[2 + 4 * steps]
    copies = []
    for k in range(steps):
        here = pl.ds(k * ar_v.shape[1] // steps, ar_v.shape[1] // steps)
        copies += place([r.at[:, k] for r in ar], masks_a, col_at, ar_v.at[:, here], sems, len(copies))
        copies.append(pltpu.make_async_copy(probe.at[k], probe_v.at[:, here], sems.at[len(copies)]))
    for copy in copies:
        copy.start()
    for copy in copies:
        copy.wait()
    masks = sum(masks_b, [])
    rows = ar_v.shape[0] // len(masks)
    for at, mask in enumerate(masks):
        start = pl.multiple_of((row_at ^ mask) * rows, 16)
        ar_out[at * rows : (at + 1) * rows, :] = ar_v[pl.ds(start, rows), :]
        probe_out[at * rows : (at + 1) * rows, :] = probe_v[pl.ds(start, rows), :]


def summed(lefts, rights):
    total = None
    for left, right in zip(lefts, rights):
        part = mm_at(left, right)
        total = part if total is None else total + part
    return total


def pieces_of(refs, which):
    x, x1, x2, l3, r3 = refs
    n, rows, width = l3.shape
    return [r[...].reshape(n * rows, width) for r in (x.at[which], x1.at[which], x2.at[which], (l3, r3)[which])]


def quarters(ref, k, width):
    rows = ref.shape[0] // 4
    return [ref[i * rows : (i + 1) * rows, k * width : (k + 1) * width] for i in range(4)]


def middle_of(scal, step, steps, ar, b):
    width = ar.shape[1] // steps
    mid = summed(quarters(ar, step, width), pieces_of(b, 0))
    weight = scal[1 + 3 * steps + step].astype(F32)
    a_rank, b_rank = scal[1 + steps + step], scal[1 + 2 * steps + step]
    return mid * rows_below(a_rank, width, width) * lanes_below(b_rank, width, width) * weight


def first_kernel(steps, scal, ar, probe, *refs):
    b, (core, cross, mid_out, rp_out, k_out, y_out, gram_out) = refs[:5], refs[5:]
    width = mid_out.shape[0]
    tmask = lanes_below(scal[1], width, width)
    k_out[:width, :] = core[0] * rows_below(scal[0], width, width) * tmask
    mid = middle_of(scal, 0, steps, ar, b)
    mid_out[...] = mid
    rows = probe.shape[0] // 4
    rp = summed(pieces_of(b, 1), [probe[i * rows : (i + 1) * rows, :] for i in range(4)])
    rp_out[...] = rp[:, width:]
    k_out[width:, :] = exact(mid, rp[:, :width] * tmask)
    k = k_out[...]
    y = exact(cross[: 2 * width, : 2 * width], k)
    y_out[...] = y
    gram_out[...] = exact_at(k, y) + unit_beyond(scal[1], width)


def inverse_kernel(tile, scal, gram, k0, y0, cross, mid0, rp01, core, w_out, core_out, h_out, t_v):
    width = gram.shape[0]
    root = math.sqrt(tile)
    w_out[...] = gram[...]

    def next_core():
        y = jnp.concatenate([y0[:width, :] * rows_below(scal[0], width, width), y0[width:, :]], 0)
        z = jnp.concatenate([core[1], exact(mid0[...], rp01[...])], 0)
        t_v[:, :width] = exact_at(y, z) * (1.0 / root)

    def next_cross():
        t_v[:, width:] = exact(cross[2 * width :, : 2 * width], k0[...]).T * root

    inverse_factor(w_out, [next_core, next_cross])
    both = exact(w_out[...], t_v[...])
    keep = rows_below(scal[1], width, width)
    core_out[...] = both[:, :width] * keep * lanes_below(scal[2], width, width)
    h_out[...] = both[:, width:] * keep


def second_kernel(
    masks_a, masks_b, steps, scal, k0, y0, w0, core_c, h0, mid0, cross, ar, probe, *refs,
):
    n = len(masks_a)
    b, refs = refs[:5], refs[5:]
    left, right, b0, b1, b2, br3, p0, p1, p2, pr3 = refs[:10]
    al, refs = refs[10 : 10 + n], refs[10 + n :]
    out_left, out_right = refs[:2]
    left_v, right_v, a_v, b_v, gram_v, k_v, q_v, outl_v, outr_v, sems, out_sems = refs[2:]
    tile, width = left_v.shape
    root = math.sqrt(tile)
    col_at, row_at = scal[1 + 4 * steps], scal[2 + 4 * steps]
    late = []
    for k, (x, x1, x2, r3) in enumerate(((p0, p1, p2, pr3), (b0, b1, b2, br3))):
        here = pl.ds(k * width, width)
        late += place((x.at[1], x1.at[1], x2.at[1], r3), masks_b, row_at, b_v.at[:, here], sems, len(late))
        late += place([r.at[:, k] for r in al], masks_a, col_at, a_v.at[:, here], sems, len(late))
    late.append(pltpu.make_async_copy(left, left_v, sems.at[len(late)]))
    late.append(pltpu.make_async_copy(right, right_v, sems.at[len(late)]))
    for copy in late:
        copy.start()
    t0, t1 = scal[1], scal[2]
    a = core_c[...]
    h = h0[...]
    h_a = exact_at(h, a)
    mid1 = middle_of(scal, 1, steps, ar, b)
    rp11 = summed(pieces_of(b, 1), quarters(probe, 1, width))
    core_b = exact(mid1, rp11 * lanes_below(t1, width, width))
    both = exact(jnp.concatenate([h, cross[2 * width :, 2 * width :]], 0), core_b)
    top = a * float(tile) + both[:width]
    low = h_a + both[width:]
    gram_v[...] = exact_at(jnp.concatenate([a, core_b], 0), jnp.concatenate([top, low], 0)) + unit_beyond(t1, width)

    def left_weights():
        k_c = close(k0[...], close_at(w0[...], a) * root)
        h, m = split2(jnp.concatenate([k_c, core_b], 0))
        k_v[...] = jnp.concatenate([h[:width], h[:width], m[:width], h[width:], m[width:]], 0)

    def right_weights():
        z = close_bt(y0[...], w0[...])
        back0 = jnp.concatenate([z[:width] * rows_below(scal[0], width, width), close_at(mid0[...], z[width:])], 0)
        q_c = close(back0, top * rows_below(t0, width, width)) * (1.0 / tile)
        h, m = split2(jnp.concatenate([q_c, close_at(mid1, low) * (1.0 / root)], 0))
        q_v[...] = jnp.concatenate([h[:width], h[:width], m[:width], h[width:], m[width:]], 0)

    def arrive():
        for copy in late:
            copy.wait()

    def form(out_v, factor, others, weights, c):
        at = slice(c * CHUNK, (c + 1) * CHUNK)
        h, m = split2(factor[at, :])
        o = others[at, :]
        out_v[at, :] = mm(jnp.concatenate([h, m, h, o, o], 1), weights[...])

    count = tile // CHUNK
    beside = [left_weights, right_weights, arrive]
    beside += [functools.partial(form, outl_v, left_v, a_v, k_v, c) for c in range(count)]
    beside += [functools.partial(form, outr_v, right_v, b_v, q_v, c) for c in range(count)]
    inverse_factor(gram_v, beside)
    h, m = split2(gram_v[...])
    weights = jnp.concatenate([h, h, m], 1)
    outs = []
    for c in range(count):
        at = pl.ds(c * CHUNK, CHUNK)
        for src, dst, scale in ((outl_v, out_left, root), (outr_v, out_right, 1.0)):
            h, m = split2(src[at, :])
            src[at, :] = mm_bt(jnp.concatenate([h, m, h], 1), weights) * scale
            copy = pltpu.make_async_copy(src.at[at, :], dst.at[at, :], out_sems.at[len(outs)])
            copy.start()
            outs.append(copy)
    for copy in outs:
        copy.wait()


def call(kernel, out_shape, in_specs, scratch, name, vmem, passes, out_space=VMEM):
    flops = passes * 2 * 2048 * 256 * 256
    return pl.pallas_call(
        kernel,
        out_shape=out_shape,
        in_specs=in_specs,
        out_specs=jax.tree.map(lambda _: pl.BlockSpec(memory_space=out_space), out_shape),
        scratch_shapes=scratch,
        compiler_params=pltpu.CompilerParams(vmem_limit_bytes=vmem * 1024 * 1024),
        cost_estimate=pl.CostEstimate(flops=flops, bytes_accessed=1 << 20, transcendentals=0),
        name=name,
    )


def on_device(
    rows_count, cols_count, c_left, c_right, c_rank, a_left, a_right, a_rank, a_pattern,
    b_left, b_right, b_rank, b_pattern, probe, target,
):
    tile, width = c_left.shape[2:]
    steps = probe.shape[0]
    left = c_left[0, 0]
    right = c_right[0, 0]
    any_, vm, sm = (pl.BlockSpec(memory_space=s) for s in (ANY, VMEM, SMEM))
    dma = pltpu.SemaphoreType.DMA

    def f32(*shape):
        return jax.ShapeDtypeStruct(shape, F32)

    scal = jnp.concatenate(
        [
            c_rank[0],
            target[0, 0],
            a_rank[0],
            b_rank[:, 0],
            a_pattern[0] * b_pattern[:, 0],
            jnp.stack([lax.axis_index("col"), lax.axis_index("row")]),
        ]
    ).astype(jnp.int32)

    whole = VMEM((tile, width), F32)
    wide = VMEM((tile, steps * width), BF16)
    a_bits = bits_of(cols_count)
    al, masks = spread(a_left, "col", cols_count, a_bits)
    ar, _ = spread(a_right, "col", cols_count, a_bits)
    masks_a = [[mask] for mask in masks]
    bits = bits_of(rows_count)
    one, two = bits[-1], bits[-2]
    core = call(
        functools.partial(probe_kernel, steps),
        f32(steps, width, width),
        [any_, any_],
        [VMEM((tile, width), F32), VMEM((tile, steps * width), BF16), dma((1 + steps,))],
        "right_probe",
        16,
        12,
    )(right, probe)
    cross = call(
        functools.partial(cross_kernel, masks_a, steps),
        f32((1 + steps) * width, (1 + steps) * width),
        [sm] + [any_] * (1 + cols_count),
        [VMEM((tile, width), F32), VMEM((tile, (2 + steps) * width), BF16), dma((1 + steps * cols_count,))],
        "left_cross",
        24,
        24,
    )(scal, left, *al)

    def own_blocks(k, *before):
        x = jnp.stack([b_left[k, 0], b_right[k, 0]])[:, None]
        return (forwarded if True else spread)(after(x, *before) if before else x, "row", rows_count, bits[:-2])

    blocks, masks = own_blocks(0)
    masks_b = [[mask ^ flip for mask in masks] for flip in (0, one, two, one ^ two)]
    ordered = call(
        functools.partial(order_kernel, masks_a, masks_b, steps),
        (jax.ShapeDtypeStruct((tile, steps * width), BF16),) * 2,
        [sm] + [any_] * (1 + cols_count),
        [wide, wide, dma((steps * (cols_count + 1),))],
        "ordered",
        20,
        5,
    )(scal, probe, *ar)
    gathered = []
    for k in range(steps):
        x = jnp.concatenate(blocks, 1)
        x = after(x, *gathered[k - 1][3:]) if k > 0 else after(x, core, al[-1])
        x1 = exchange(x, "row", rows_count, one)
        x2 = exchange(x, "row", rows_count, two)
        before = ()
        if k == 0:
            blocks, _ = own_blocks(1, x)
            before = (cross, *ordered)
        l3 = exchange(after(x1[0], *before), "row", rows_count, two)
        r3 = exchange(after(x2[1], *before), "row", rows_count, one)
        gathered.append((x, x1, x2, l3, r3))

    mid0, rp01, k0, y0, gram = call(
        functools.partial(first_kernel, steps),
        (f32(width, width), f32(width, width), f32(2 * width, width), f32(2 * width, width), f32(width, width)),
        [sm] + [vm] * 9,
        [],
        "first_step",
        20,
        20,
    )(scal, *ordered, *gathered[0], core, cross)
    w0, core_c, h0 = call(
        functools.partial(inverse_kernel, tile),
        (f32(width, width),) * 3,
        [sm] + [vm] * 7,
        [VMEM((width, 2 * width), F32)],
        "inverse_factor",
        24,
        30,
    )(scal, gram, k0, y0, cross, mid0, rp01, core)
    weights = VMEM(((3 + 2 * steps) * width, width), BF16)
    late_b = [g[i] for g in (gathered[1], gathered[0]) for i in (0, 1, 2, 4)]
    out_left, out_right = call(
        functools.partial(second_kernel, masks_a, masks_b, steps),
        (f32(tile, width), f32(tile, width)),
        [sm] + [vm] * 14 + [any_] * (10 + cols_count),
        [
            whole, whole, wide, wide, VMEM((width, width), F32), weights, weights, whole, whole,
            dma((2 * rows_count + steps * cols_count + 2,)), dma((2 * (tile // CHUNK),)),
        ],
        "second_step",
        36,
        100,
        ANY,
    )(scal, k0, y0, w0, core_c, h0, mid0, cross, *ordered, *gathered[1], left, right, *late_b, *al)
    return (out_left[None, None], out_right[None, None])


def solution(mesh):
    return jax.shard_map(
        functools.partial(on_device, mesh.shape["row"], mesh.shape["col"]),
        mesh=mesh,
        in_specs=(
            P("row", "col", None, None),
            P("row", "col", None, None),
            P("row", "col"),
            P("row", None, "col", None),
            P("row", None, "col", None),
            P("row", None),
            P("row", None),
            P(None, "col", "row", None),
            P(None, "col", "row", None),
            P(None, "col"),
            P(None, "col"),
            P(),
            P("row", "col", None),
        ),
        out_specs=(P("row", "col", None, None), P("row", "col", None, None)),
        check_vma=False,
    )
```

profile of v0, /device:TPU:0, one launch (start us, length us, event | category | flops | bytes accessed | tf_op | source)
XLA Modules:
  0.0 85.2 jit_solution(6189761024835469136)
XLA Ops:
  0.6 0.5 collective-permute-start.4
  1.1 1.0 %slice_bitcast_fusion.4 = (bf16[1,128,256]{2,1,0:T(8,128)(2,1)S(1)}, bf16[1,128,256]{2,1,0:T(8,128)(2,1)S(1)}, bf16[1,128,256]{2,1,0:T(8,128)(2,1)S(1)}, bf16[1,128,256]{2,1,0:T(8,128)(2,1)S(1)}) fusion(bf16[2,1,128,256]{3,2,1,0:T(8,128)(2,1)} %param.21, bf16[2,1,128,256]{3,2,1,0:T(8,128)(2,1)} %param.20), kind=kLoop, calls=%fused_computation.8 | loop fusion | bytes 524288 | tf_op jit(solution)/shard_map/stack;squeeze | solution.py:476
  2.1 2.7 %collective-permute-start.2 = (bf16[2,1,128,256]{3,2,1,0:T(8,128)(2,1)S(1)}, bf16[2,1,128,256]{3,2,1,0:T(8,128)(2,1)S(1)}, u32[]{:S(2)}, u32[]{:S(2)}) collective-permute-start(bf16[2,1,128,256]{3,2,1,0:T(8,128)(2,1)S(1)} %maximum_bitcast_fusion), channel_id=1, source_target_pairs={{0,8},{2,10},{4,12},{6,14},{8,0},{10,2},{12,4},{14,6},{16,24},{18,... | collective-permute-start | bytes 393224 | tf_op jit(solution)/shard_map/ppermute | solution.py:21
  4.8 2.6 %collective-permute-start.1 = (bf16[2,1,128,256]{3,2,1,0:T(8,128)(2,1)S(1)}, bf16[2,1,128,256]{3,2,1,0:T(8,128)(2,1)}, u32[]{:S(2)}, u32[]{:S(2)}) collective-permute-start(bf16[2,1,128,256]{3,2,1,0:T(8,128)(2,1)S(1)} %maximum_bitcast_fusion), channel_id=1, source_target_pairs={{0,16},{2,18},{4,20},{6,22},{8,24},{10,26},{12,28},{14,30},{16,0},... | collective-permute-start | bytes 393224 | tf_op jit(solution)/shard_map/ppermute | solution.py:21
  7.4 0.0 collective-permute-start
  7.4 1.6 %copy-done = bf16[2,2048,256]{2,1,0:T(8,128)(2,1)S(1)} copy-done((bf16[2,2048,256]{2,1,0:T(8,128)(2,1)S(1)}, bf16[2,2048,256]{2,1,0:T(8,128)(2,1)}, u32[]{:S(2)}) %copy-start) | copy-done | bytes 2097176
  9.0 1.6 %copy-done.2 = f32[1,1,2048,256]{3,2,1,0:T(8,128)S(1)} copy-done((f32[1,1,2048,256]{3,2,1,0:T(8,128)S(1)}, f32[1,1,2048,256]{3,2,1,0:T(8,128)}, u32[]{:S(2)}) %copy-start.2) | copy-done | bytes 2097176
  10.6 0.0 copy-start.12
  10.6 0.0 copy-start.4
  10.6 0.0 copy-start.6
  10.6 1.6 %right_probe.1.refs_5_.core = f32[2,256,256]{2,1,0:T(8,128)S(1)} custom-call(f32[2048,256]{1,0:T(8,128)S(1)} %bitcast.35, bf16[2,2048,256]{2,1,0:T(8,128)(2,1)S(1)} %copy-done), custom_call_target="tpu_custom_call" | custom-call | flops 3221225472 | bytes 1048576 | tf_op jit(solution)/shard_map/right_probe/pallas_call | solution.py:456
  12.2 0.0 copy-start.8
  12.3 0.8 copy-done.8
  13.0 1.2 %collective-permute-done.1 = bf16[2,1,128,256]{3,2,1,0:T(8,128)(2,1)} collective-permute-done((bf16[2,1,128,256]{3,2,1,0:T(8,128)(2,1)S(1)}, bf16[2,1,128,256]{3,2,1,0:T(8,128)(2,1)}, u32[]{:S(2)}, u32[]{:S(2)}) %collective-permute-start.1) | collective-permute-done | bytes 131104 | tf_op jit(solution)/shard_map/ppermute | solution.py:21
  14.3 0.4 collective-permute-start.3
  14.7 0.5 bitcast_multiply_fusion
  15.9 0.7 concatenate.9.scal
  16.6 0.0 collective-permute-done.2
  16.7 2.9 %collective-permute-done.3 = bf16[2,1,128,256]{3,2,1,0:T(8,128)(2,1)} collective-permute-done((bf16[2,1,128,256]{3,2,1,0:T(8,128)(2,1)}, bf16[2,1,128,256]{3,2,1,0:T(8,128)(2,1)}, u32[]{:S(2)}, u32[]{:S(2)}) %collective-permute-start.3) | collective-permute-done | bytes 131104 | tf_op jit(solution)/shard_map/ppermute | solution.py:21
  19.5 1.0 %pad_maximum_fusion.refs_0_.refs_11_ = bf16[2,4,128,256]{3,2,1,0:T(8,128)(2,1)S(1)} fusion(bf16[2,1,128,256]{3,2,1,0:T(8,128)(2,1)} %collective-permute-done.3, bf16[2,1,128,256]{3,2,1,0:T(8,128)(2,1)S(1)} %collective-permute-done.2, bf16[2,1,128,256]{3,2,1,0:T(8,128)(2,1)} %collective-permute-done.1, bf16[2,1,128,256]{3,2,1,0:T(8,128)(2,1)S(1)} %maximum_bitcast_fusion), kind=kLoop, calls=%fused_computation | loop fusion | flops 786432 | bytes 1048576 | tf_op jit(solution)/shard_map/concatenate | solution.py:492
  20.6 0.0 collective-permute-done.4.refs_1_.refs_16_
  20.6 1.6 %collective-permute-start.6 = (bf16[2,4,128,256]{3,2,1,0:T(8,128)(2,1)S(1)}, bf16[2,4,128,256]{3,2,1,0:T(8,128)(2,1)S(1)}, u32[]{:S(2)}, u32[]{:S(2)}) collective-permute-start(bf16[2,4,128,256]{3,2,1,0:T(8,128)(2,1)S(1)} %pad_maximum_fusion.refs_0_.refs_11_), channel_id=1, source_target_pairs={{0,4},{2,6},{4,0},{6,2},{8,12},{10,14},{12,8},{14,10},{16,20},{18,... | collective-permute-start | bytes 1572872 | tf_op jit(solution)/shard_map/ppermute | solution.py:21
  22.2 1.5 %collective-permute-start.5 = (bf16[2,4,128,256]{3,2,1,0:T(8,128)(2,1)S(1)}, bf16[2,4,128,256]{3,2,1,0:T(8,128)(2,1)S(1)}, u32[]{:S(2)}, u32[]{:S(2)}) collective-permute-start(bf16[2,4,128,256]{3,2,1,0:T(8,128)(2,1)S(1)} %pad_maximum_fusion.refs_0_.refs_11_), channel_id=1, source_target_pairs={{0,2},{2,0},{4,6},{6,4},{8,10},{10,8},{12,14},{14,12},{16,18},{18,... | collective-permute-start | bytes 1572872 | tf_op jit(solution)/shard_map/ppermute | solution.py:21
  23.7 1.1 %collective-permute-start.9 = (bf16[2,1,128,256]{3,2,1,0:T(8,128)(2,1)S(1)}, bf16[2,1,128,256]{3,2,1,0:T(8,128)(2,1)S(1)}, u32[]{:S(2)}, u32[]{:S(2)}) collective-permute-start(bf16[2,1,128,256]{3,2,1,0:T(8,128)(2,1)S(1)} %maximum_bitcast_fusion.1), channel_id=1, source_target_pairs={{0,16},{2,18},{4,20},{6,22},{8,24},{10,26},{12,28},{14,30},{16,0},... | collective-permute-start | bytes 393224 | tf_op jit(solution)/shard_map/ppermute | solution.py:21
  24.8 5.6 %left_cross.1.refs_6_.cross = f32[768,768]{1,0:T(8,128)S(1)} custom-call(s32[11]{0:T(128)S(1)} %concatenate.9.scal, f32[2048,256]{1,0:T(8,128)S(1)} %bitcast.37, bf16[1,2,1024,256]{3,2,1,0:T(8,128)(2,1)S(1)} %copy-done.6, bf16[1,2,1024,256]{3,2,1,0:T(8,128)(2,1)} %collective-permute-done.4.refs_1_.refs_16_), custom_call_target="tpu_custom_call" | custom-call | flops 6442450944 | bytes 1048576 | tf_op jit(solution)/shard_map/left_cross/pallas_call | solution.py:465
  30.4 0.0 collective-permute-done.refs_1_
  30.4 2.3 %ordered.1 = (bf16[2048,512]{1,0:T(8,128)(2,1)S(1)}, bf16[2048,512]{1,0:T(8,128)(2,1)S(1)}) custom-call(s32[11]{0:T(128)S(1)} %concatenate.9.scal, bf16[2,2048,256]{2,1,0:T(8,128)(2,1)S(1)} %copy-done.1, bf16[1,2,1024,256]{3,2,1,0:T(8,128)(2,1)S(1)} %copy-done.5, bf16[1,2,1024,256]{3,2,1,0:T(8,128)(2,1)} %collective-permute-done.refs_1_), custom_call_target="tpu_custom_call" | custom-call | flops 1342177280 | bytes 1048576 | tf_op jit(solution)/shard_map/ordered/pallas_call | solution.py:481
  32.7 0.0 copy-start.9
  32.7 0.0 collective-permute-done.6.refs_2_.refs_13_
  32.8 1.1 %collective-permute-done.5.refs_1_.refs_12_ = bf16[2,4,128,256]{3,2,1,0:T(8,128)(2,1)S(1)} collective-permute-done((bf16[2,4,128,256]{3,2,1,0:T(8,128)(2,1)S(1)}, bf16[2,4,128,256]{3,2,1,0:T(8,128)(2,1)S(1)}, u32[]{:S(2)}, u32[]{:S(2)}) %collective-permute-start.5) | collective-permute-done | bytes 524320 | tf_op jit(solution)/shard_map/ppermute | solution.py:21
  33.9 0.6 collective-permute-start.7
  34.5 1.5 %collective-permute-start.8 = (bf16[4,128,256]{2,1,0:T(8,128)(2,1)S(1)}, bf16[4,128,256]{2,1,0:T(8,128)(2,1)S(1)}, u32[]{:S(2)}, u32[]{:S(2)}) collective-permute-start(bf16[4,128,256]{2,1,0:T(8,128)(2,1)S(1)} %slice_bitcast_fusion.2), channel_id=1, source_target_pairs={{0,2},{2,0},{4,6},{6,4},{8,10},{10,8},{12,14},{14,12},{16,18},{18,... | collective-permute-start | bytes 786440 | tf_op jit(solution)/shard_map/ppermute | solution.py:21
  35.9 1.2 %collective-permute-start.10 = (bf16[2,1,128,256]{3,2,1,0:T(8,128)(2,1)S(1)}, bf16[2,1,128,256]{3,2,1,0:T(8,128)(2,1)S(1)}, u32[]{:S(2)}, u32[]{:S(2)}) collective-permute-start(bf16[2,1,128,256]{3,2,1,0:T(8,128)(2,1)S(1)} %maximum_bitcast_fusion.1), channel_id=1, source_target_pairs={{0,8},{2,10},{4,12},{6,14},{8,0},{10,2},{12,4},{14,6},{16,24},{18,... | collective-permute-start | bytes 393224 | tf_op jit(solution)/shard_map/ppermute | solution.py:21
  37.1 0.0 collective-permute-done.9
  37.1 0.9 %collective-permute-start.11 = (bf16[2,1,128,256]{3,2,1,0:T(8,128)(2,1)S(1)}, bf16[2,1,128,256]{3,2,1,0:T(8,128)(2,1)S(1)}, u32[]{:S(2)}, u32[]{:S(2)}) collective-permute-start(bf16[2,1,128,256]{3,2,1,0:T(8,128)(2,1)S(1)} %collective-permute-done.9), channel_id=1, source_target_pairs={{0,8},{2,10},{4,12},{6,14},{8,0},{10,2},{12,4},{14,6},{16,24},{18,... | collective-permute-start | bytes 393224 | tf_op jit(solution)/shard_map/ppermute | solution.py:21
  38.0 2.9 %collective-permute-done.10 = bf16[2,1,128,256]{3,2,1,0:T(8,128)(2,1)S(1)} collective-permute-done((bf16[2,1,128,256]{3,2,1,0:T(8,128)(2,1)S(1)}, bf16[2,1,128,256]{3,2,1,0:T(8,128)(2,1)S(1)}, u32[]{:S(2)}, u32[]{:S(2)}) %collective-permute-start.10) | collective-permute-done | bytes 131104 | tf_op jit(solution)/shard_map/ppermute | solution.py:21
  40.9 1.4 %collective-permute-done.11 = bf16[2,1,128,256]{3,2,1,0:T(8,128)(2,1)S(1)} collective-permute-done((bf16[2,1,128,256]{3,2,1,0:T(8,128)(2,1)S(1)}, bf16[2,1,128,256]{3,2,1,0:T(8,128)(2,1)S(1)}, u32[]{:S(2)}, u32[]{:S(2)}) %collective-permute-start.11) | collective-permute-done | bytes 131104 | tf_op jit(solution)/shard_map/ppermute | solution.py:21
  42.3 0.1 pad_maximum_fusion.1.refs_0_.refs_7_
  42.4 0.0 collective-permute-done.8.refs_4_.refs_14_
  42.4 1.6 %collective-permute-start.13 = (bf16[2,4,128,256]{3,2,1,0:T(8,128)(2,1)S(1)}, bf16[2,4,128,256]{3,2,1,0:T(8,128)(2,1)S(1)}, u32[]{:S(2)}, u32[]{:S(2)}) collective-permute-start(bf16[2,4,128,256]{3,2,1,0:T(8,128)(2,1)S(1)} %pad_maximum_fusion.1.refs_0_.refs_7_), channel_id=1, source_target_pairs={{0,4},{2,6},{4,0},{6,2},{8,12},{10,14},{12,8},{14,10},{16,20},{18,... | collective-permute-start | bytes 1572872 | tf_op jit(solution)/shard_map/ppermute | solution.py:21
  44.0 0.8 collective-permute-start.12
  44.8 4.6 %first_step.1 = (f32[256,256]{1,0:T(8,128)S(1)}, f32[256,256]{1,0:T(8,128)S(1)}, f32[512,256]{1,0:T(8,128)S(1)}, f32[512,256]{1,0:T(8,128)S(1)}, f32[256,256]{1,0:T(8,128)S(1)}) custom-call(s32[11]{0:T(128)S(1)} %concatenate.9.scal, bf16[2048,512]{1,0:T(8,128)(2,1)S(1)} %get-tuple-element.19.ar, bf16[2048,512]{1,0:T(8,128)(2,1)S(1)} %get-tuple-element.20.probe, ...), custom_call_target="tpu_custom_call" | custom-call | flops 5368709120 | bytes 1048576 | tf_op jit(solution)/shard_map/first_step/pallas_call | solution.py:504
  49.4 3.8 %collective-permute-done.13.refs_2_.refs_9_ = bf16[2,4,128,256]{3,2,1,0:T(8,128)(2,1)S(1)} collective-permute-done((bf16[2,4,128,256]{3,2,1,0:T(8,128)(2,1)S(1)}, bf16[2,4,128,256]{3,2,1,0:T(8,128)(2,1)S(1)}, u32[]{:S(2)}, u32[]{:S(2)}) %collective-permute-start.13) | collective-permute-done | bytes 524320 | tf_op jit(solution)/shard_map/ppermute | solution.py:21
  53.2 1.6 %collective-permute-start.15 = (bf16[4,128,256]{2,1,0:T(8,128)(2,1)S(1)}, bf16[4,128,256]{2,1,0:T(8,128)(2,1)S(1)}, u32[]{:S(2)}, u32[]{:S(2)}) collective-permute-start(bf16[4,128,256]{2,1,0:T(8,128)(2,1)S(1)} %slice_bitcast_fusion), channel_id=1, source_target_pairs={{0,2},{2,0},{4,6},{6,4},{8,10},{10,8},{12,14},{14,12},{16,18},{18,... | collective-permute-start | bytes 786440 | tf_op jit(solution)/shard_map/ppermute | solution.py:21
  54.8 1.2 %collective-permute-done.12.refs_1_.refs_8_ = bf16[2,4,128,256]{3,2,1,0:T(8,128)(2,1)S(1)} collective-permute-done((bf16[2,4,128,256]{3,2,1,0:T(8,128)(2,1)S(1)}, bf16[2,4,128,256]{3,2,1,0:T(8,128)(2,1)S(1)}, u32[]{:S(2)}, u32[]{:S(2)}) %collective-permute-start.12) | collective-permute-done | bytes 524320 | tf_op jit(solution)/shard_map/ppermute | solution.py:21
  56.0 0.6 collective-permute-start.14
  56.7 9.8 %inverse_factor.1 = (f32[256,256]{1,0:T(8,128)S(1)}, f32[256,256]{1,0:T(8,128)S(1)}, f32[256,256]{1,0:T(8,128)S(1)}) custom-call(s32[11]{0:T(128)S(1)} %concatenate.9.scal, f32[256,256]{1,0:T(8,128)S(1)} %get-tuple-element.26.gram, f32[512,256]{1,0:T(8,128)S(1)} %get-tuple-element.24.k0, f32[512,256]{1,0:T(8,128)S(1)} %get-tuple-element.25.y0, ...), custom_call_target="tpu_custom_call" | custom-call | flops 8053063680 | bytes 1048576 | tf_op jit(solution)/shard_map/inverse_factor/pallas_call | solution.py:513
  66.5 18.6 %second_step.1 = (f32[2048,256]{1,0:T(8,128)}, f32[2048,256]{1,0:T(8,128)}) custom-call(s32[11]{0:T(128)S(1)} %concatenate.9.scal, f32[512,256]{1,0:T(8,128)S(1)} %get-tuple-element.24.k0, f32[512,256]{1,0:T(8,128)S(1)} %get-tuple-element.25.y0, f32[256,256]{1,0:T(8,128)S(1)} %get-tuple-element.29.w0, f32[256,256]{1,0:T(8,128)S(1)} %get-tuple-element.30.core_c, ...), custom_call_target="tpu_custom_call" | custom-call | flops 26843545600 | bytes 1048576 | tf_op jit(solution)/shard_map/second_step/pallas_call | solution.py:524
  (31 shorter events, 0.2 us)
Async XLA Ops:
  0.6 20.0 %collective-permute-start.4 = (bf16[1,2,1024,256]{3,2,1,0:T(8,128)(2,1)}, bf16[1,2,1024,256]{3,2,1,0:T(8,128)(2,1)}, u32[]{:S(2)}, u32[]{:S(2)}) collective-permute-start(bf16[1,2,1024,256]{3,2,1,0:T(8,128)(2,1)} %refs_15_.1), channel_id=1, source_target_pairs={{0,1},{1,0},{2,3},{3,2},{4,5},{5,4},{6,7},{7,6},{8,9},{9,8},{10,11... | collective-permute-start | bytes 3145736 | tf_op jit(solution)/shard_map/ppermute | solution.py:21
  2.1 14.5 %collective-permute-start.2 = (bf16[2,1,128,256]{3,2,1,0:T(8,128)(2,1)S(1)}, bf16[2,1,128,256]{3,2,1,0:T(8,128)(2,1)S(1)}, u32[]{:S(2)}, u32[]{:S(2)}) collective-permute-start(bf16[2,1,128,256]{3,2,1,0:T(8,128)(2,1)S(1)} %maximum_bitcast_fusion), channel_id=1, source_target_pairs={{0,8},{2,10},{4,12},{6,14},{8,0},{10,2},{12,4},{14,6},{16,24},{18,... | collective-permute-start | bytes 393224 | tf_op jit(solution)/shard_map/ppermute | solution.py:21
  4.8 9.5 %collective-permute-start.1 = (bf16[2,1,128,256]{3,2,1,0:T(8,128)(2,1)S(1)}, bf16[2,1,128,256]{3,2,1,0:T(8,128)(2,1)}, u32[]{:S(2)}, u32[]{:S(2)}) collective-permute-start(bf16[2,1,128,256]{3,2,1,0:T(8,128)(2,1)S(1)} %maximum_bitcast_fusion), channel_id=1, source_target_pairs={{0,16},{2,18},{4,20},{6,22},{8,24},{10,26},{12,28},{14,30},{16,0},... | collective-permute-start | bytes 393224 | tf_op jit(solution)/shard_map/ppermute | solution.py:21
  7.4 23.0 %collective-permute-start = (bf16[1,2,1024,256]{3,2,1,0:T(8,128)(2,1)}, bf16[1,2,1024,256]{3,2,1,0:T(8,128)(2,1)}, u32[]{:S(2)}, u32[]{:S(2)}) collective-permute-start(bf16[1,2,1024,256]{3,2,1,0:T(8,128)(2,1)} %refs_0_.2), channel_id=1, source_target_pairs={{0,1},{1,0},{2,3},{3,2},{4,5},{5,4},{6,7},{7,6},{8,9},{9,8},{10,11... | collective-permute-start | bytes 3145736 | tf_op jit(solution)/shard_map/ppermute | solution.py:21
  7.4 1.6 %copy-start = (bf16[2,2048,256]{2,1,0:T(8,128)(2,1)S(1)}, bf16[2,2048,256]{2,1,0:T(8,128)(2,1)}, u32[]{:S(2)}) copy-start(bf16[2,2048,256]{2,1,0:T(8,128)(2,1)} %probe.3) | copy-start | bytes 6291460
  9.0 1.6 %copy-start.2 = (f32[1,1,2048,256]{3,2,1,0:T(8,128)S(1)}, f32[1,1,2048,256]{3,2,1,0:T(8,128)}, u32[]{:S(2)}) copy-start(f32[1,1,2048,256]{3,2,1,0:T(8,128)} %param.14) | copy-start | bytes 6291460
  10.6 4.1 %copy-start.13 = (s32[2,1]{0,1:T(1,128)S(1)}, s32[2,1]{0,1:T(1,128)}, u32[]{:S(2)}) copy-start(s32[2,1]{0,1:T(1,128)} %param.23) | copy-start | bytes 28
  10.6 4.1 %copy-start.14 = (s32[1,2]{1,0:T(1,128)S(1)}, s32[1,2]{1,0:T(1,128)}, u32[]{:S(2)}) copy-start(s32[1,2]{1,0:T(1,128)} %param.19) | copy-start | bytes 28
  10.6 5.3 %copy-start.10 = (s32[1,1,2]{2,1,0:T(1,128)S(1)}, s32[1,1,2]{2,1,0:T(1,128)}, u32[]{:S(2)}) copy-start(s32[1,1,2]{2,1,0:T(1,128)} %param.25) | copy-start | bytes 28
  10.6 5.3 %copy-start.11 = (s32[1,2]{1,0:T(1,128)S(1)}, s32[1,2]{1,0:T(1,128)}, u32[]{:S(2)}) copy-start(s32[1,2]{1,0:T(1,128)} %param.18) | copy-start | bytes 28
  10.6 5.4 %copy-start.12 = (s32[2,1]{0,1:T(1,128)S(1)}, s32[2,1]{0,1:T(1,128)}, u32[]{:S(2)}) copy-start(s32[2,1]{0,1:T(1,128)} %param.22) | copy-start | bytes 28
  10.6 14.2 %copy-start.4 = (f32[1,1,2048,256]{3,2,1,0:T(8,128)S(1)}, f32[1,1,2048,256]{3,2,1,0:T(8,128)}, u32[]{:S(2)}) copy-start(f32[1,1,2048,256]{3,2,1,0:T(8,128)} %param.13) | copy-start | bytes 6291460
  10.6 14.2 %copy-start.6 = (bf16[1,2,1024,256]{3,2,1,0:T(8,128)(2,1)S(1)}, bf16[1,2,1024,256]{3,2,1,0:T(8,128)(2,1)}, u32[]{:S(2)}) copy-start(bf16[1,2,1024,256]{3,2,1,0:T(8,128)(2,1)} %refs_15_.1) | copy-start | bytes 3145732
  12.2 0.8 copy-start.8
  14.3 5.3 %collective-permute-start.3 = (bf16[2,1,128,256]{3,2,1,0:T(8,128)(2,1)}, bf16[2,1,128,256]{3,2,1,0:T(8,128)(2,1)}, u32[]{:S(2)}, u32[]{:S(2)}) collective-permute-start(bf16[2,1,128,256]{3,2,1,0:T(8,128)(2,1)} %collective-permute-done.1), channel_id=1, source_target_pairs={{0,8},{2,10},{4,12},{6,14},{8,0},{10,2},{12,4},{14,6},{16,24},{18,... | collective-permute-start | bytes 393224 | tf_op jit(solution)/shard_map/ppermute | solution.py:21
  20.6 12.1 %collective-permute-start.6 = (bf16[2,4,128,256]{3,2,1,0:T(8,128)(2,1)S(1)}, bf16[2,4,128,256]{3,2,1,0:T(8,128)(2,1)S(1)}, u32[]{:S(2)}, u32[]{:S(2)}) collective-permute-start(bf16[2,4,128,256]{3,2,1,0:T(8,128)(2,1)S(1)} %pad_maximum_fusion.refs_0_.refs_11_), channel_id=1, source_target_pairs={{0,4},{2,6},{4,0},{6,2},{8,12},{10,14},{12,8},{14,10},{16,20},{18,... | collective-permute-start | bytes 1572872 | tf_op jit(solution)/shard_map/ppermute | solution.py:21
  22.2 11.7 %collective-permute-start.5 = (bf16[2,4,128,256]{3,2,1,0:T(8,128)(2,1)S(1)}, bf16[2,4,128,256]{3,2,1,0:T(8,128)(2,1)S(1)}, u32[]{:S(2)}, u32[]{:S(2)}) collective-permute-start(bf16[2,4,128,256]{3,2,1,0:T(8,128)(2,1)S(1)} %pad_maximum_fusion.refs_0_.refs_11_), channel_id=1, source_target_pairs={{0,2},{2,0},{4,6},{6,4},{8,10},{10,8},{12,14},{14,12},{16,18},{18,... | collective-permute-start | bytes 1572872 | tf_op jit(solution)/shard_map/ppermute | solution.py:21
  23.7 13.4 %collective-permute-start.9 = (bf16[2,1,128,256]{3,2,1,0:T(8,128)(2,1)S(1)}, bf16[2,1,128,256]{3,2,1,0:T(8,128)(2,1)S(1)}, u32[]{:S(2)}, u32[]{:S(2)}) collective-permute-start(bf16[2,1,128,256]{3,2,1,0:T(8,128)(2,1)S(1)} %maximum_bitcast_fusion.1), channel_id=1, source_target_pairs={{0,16},{2,18},{4,20},{6,22},{8,24},{10,26},{12,28},{14,30},{16,0},... | collective-permute-start | bytes 393224 | tf_op jit(solution)/shard_map/ppermute | solution.py:21
  24.8 5.6 %copy-start.1 = (bf16[2,2048,256]{2,1,0:T(8,128)(2,1)S(1)}, bf16[2,2048,256]{2,1,0:T(8,128)(2,1)}, u32[]{:S(2)}) copy-start(bf16[2,2048,256]{2,1,0:T(8,128)(2,1)} %probe.3) | copy-start | bytes 6291460
  24.8 5.6 %copy-start.5 = (bf16[1,2,1024,256]{3,2,1,0:T(8,128)(2,1)S(1)}, bf16[1,2,1024,256]{3,2,1,0:T(8,128)(2,1)}, u32[]{:S(2)}) copy-start(bf16[1,2,1024,256]{3,2,1,0:T(8,128)(2,1)} %refs_0_.2) | copy-start | bytes 3145732
  30.4 26.3 %copy-start.7 = (f32[768,768]{1,0:T(8,128)}, f32[768,768]{1,0:T(8,128)S(1)}, u32[]{:S(2)}) copy-start(f32[768,768]{1,0:T(8,128)S(1)} %left_cross.1.refs_6_.cross) | copy-start | bytes 7077892
  32.7 12.1 %copy-start.9 = (f32[2,256,256]{2,1,0:T(8,128)S(1)}, f32[2,256,256]{2,1,0:T(8,128)}, u32[]{:S(2)}) copy-start(f32[2,256,256]{2,1,0:T(8,128)} %copy-done.8) | copy-start | bytes 1572868
  33.9 8.5 %collective-permute-start.7 = (bf16[4,128,256]{2,1,0:T(8,128)(2,1)S(1)}, bf16[4,128,256]{2,1,0:T(8,128)(2,1)S(1)}, u32[]{:S(2)}, u32[]{:S(2)}) collective-permute-start(bf16[4,128,256]{2,1,0:T(8,128)(2,1)S(1)} %slice_bitcast_fusion.3), channel_id=1, source_target_pairs={{0,4},{2,6},{4,0},{6,2},{8,12},{10,14},{12,8},{14,10},{16,20},{18,... | collective-permute-start | bytes 786440 | tf_op jit(solution)/shard_map/ppermute | solution.py:21
  34.5 7.9 %collective-permute-start.8 = (bf16[4,128,256]{2,1,0:T(8,128)(2,1)S(1)}, bf16[4,128,256]{2,1,0:T(8,128)(2,1)S(1)}, u32[]{:S(2)}, u32[]{:S(2)}) collective-permute-start(bf16[4,128,256]{2,1,0:T(8,128)(2,1)S(1)} %slice_bitcast_fusion.2), channel_id=1, source_target_pairs={{0,2},{2,0},{4,6},{6,4},{8,10},{10,8},{12,14},{14,12},{16,18},{18,... | collective-permute-start | bytes 786440 | tf_op jit(solution)/shard_map/ppermute | solution.py:21
  35.9 5.0 %collective-permute-start.10 = (bf16[2,1,128,256]{3,2,1,0:T(8,128)(2,1)S(1)}, bf16[2,1,128,256]{3,2,1,0:T(8,128)(2,1)S(1)}, u32[]{:S(2)}, u32[]{:S(2)}) collective-permute-start(bf16[2,1,128,256]{3,2,1,0:T(8,128)(2,1)S(1)} %maximum_bitcast_fusion.1), channel_id=1, source_target_pairs={{0,8},{2,10},{4,12},{6,14},{8,0},{10,2},{12,4},{14,6},{16,24},{18,... | collective-permute-start | bytes 393224 | tf_op jit(solution)/shard_map/ppermute | solution.py:21
  37.1 5.2 %collective-permute-start.11 = (bf16[2,1,128,256]{3,2,1,0:T(8,128)(2,1)S(1)}, bf16[2,1,128,256]{3,2,1,0:T(8,128)(2,1)S(1)}, u32[]{:S(2)}, u32[]{:S(2)}) collective-permute-start(bf16[2,1,128,256]{3,2,1,0:T(8,128)(2,1)S(1)} %collective-permute-done.9), channel_id=1, source_target_pairs={{0,8},{2,10},{4,12},{6,14},{8,0},{10,2},{12,4},{14,6},{16,24},{18,... | collective-permute-start | bytes 393224 | tf_op jit(solution)/shard_map/ppermute | solution.py:21
  42.4 10.8 %collective-permute-start.13 = (bf16[2,4,128,256]{3,2,1,0:T(8,128)(2,1)S(1)}, bf16[2,4,128,256]{3,2,1,0:T(8,128)(2,1)S(1)}, u32[]{:S(2)}, u32[]{:S(2)}) collective-permute-start(bf16[2,4,128,256]{3,2,1,0:T(8,128)(2,1)S(1)} %pad_maximum_fusion.1.refs_0_.refs_7_), channel_id=1, source_target_pairs={{0,4},{2,6},{4,0},{6,2},{8,12},{10,14},{12,8},{14,10},{16,20},{18,... | collective-permute-start | bytes 1572872 | tf_op jit(solution)/shard_map/ppermute | solution.py:21
  44.0 12.0 %collective-permute-start.12 = (bf16[2,4,128,256]{3,2,1,0:T(8,128)(2,1)S(1)}, bf16[2,4,128,256]{3,2,1,0:T(8,128)(2,1)S(1)}, u32[]{:S(2)}, u32[]{:S(2)}) collective-permute-start(bf16[2,4,128,256]{3,2,1,0:T(8,128)(2,1)S(1)} %pad_maximum_fusion.1.refs_0_.refs_7_), channel_id=1, source_target_pairs={{0,2},{2,0},{4,6},{6,4},{8,10},{10,8},{12,14},{14,12},{16,18},{18,... | collective-permute-start | bytes 1572872 | tf_op jit(solution)/shard_map/ppermute | solution.py:21
  53.2 13.2 %collective-permute-start.15 = (bf16[4,128,256]{2,1,0:T(8,128)(2,1)S(1)}, bf16[4,128,256]{2,1,0:T(8,128)(2,1)S(1)}, u32[]{:S(2)}, u32[]{:S(2)}) collective-permute-start(bf16[4,128,256]{2,1,0:T(8,128)(2,1)S(1)} %slice_bitcast_fusion), channel_id=1, source_target_pairs={{0,2},{2,0},{4,6},{6,4},{8,10},{10,8},{12,14},{14,12},{16,18},{18,... | collective-permute-start | bytes 786440 | tf_op jit(solution)/shard_map/ppermute | solution.py:21
  56.0 10.4 %collective-permute-start.14 = (bf16[4,128,256]{2,1,0:T(8,128)(2,1)S(1)}, bf16[4,128,256]{2,1,0:T(8,128)(2,1)S(1)}, u32[]{:S(2)}, u32[]{:S(2)}) collective-permute-start(bf16[4,128,256]{2,1,0:T(8,128)(2,1)S(1)} %slice_bitcast_fusion.1), channel_id=1, source_target_pairs={{0,4},{2,6},{4,0},{6,2},{8,12},{10,14},{12,8},{14,10},{16,20},{18,... | collective-permute-start | bytes 786440 | tf_op jit(solution)/shard_map/ppermute | solution.py:21
  56.7 9.8 %copy-start.3 = (f32[1,1,2048,256]{3,2,1,0:T(8,128)S(1)}, f32[1,1,2048,256]{3,2,1,0:T(8,128)}, u32[]{:S(2)}) copy-start(f32[1,1,2048,256]{3,2,1,0:T(8,128)} %param.14) | copy-start | bytes 6291460
where the time goes:
time: 85.6 us; the launch traced here: 85.2 us
  Pallas kernels  42.4 us (50%)
  starting transfers between devices  19.1 us (22%)
  waiting for transfers between devices  14.6 us (17%)
  local copies, waits for them, and re-layouts  5.75 us (7%)
  between operations  1.73 us (2%)
  other arithmetic  1.67 us (2%)
    ppermute x16, starting transfers between devices, exchange(): return lax.ppermute(x, axis, [(r, r ^ bit) for r in range(size)])  19.1 us
    pallas_call x1, Pallas kernels, on_device(): call(functools.partial(second_kernel, masks_a, masks_b, steps), (f32(tile...  18.6 us
    ppermute x16, waiting for transfers between devices, exchange(): return lax.ppermute(x, axis, [(r, r ^ bit) for r in range(size)])  14.6 us
    pallas_call x1, Pallas kernels, on_device(): call(functools.partial(inverse_kernel, tile), (f32(width, width),) * 3, [...  9.76 us
    pallas_call x1, Pallas kernels, on_device(): call(functools.partial(cross_kernel, masks_a, steps), f32((1 + steps) * w...  5.55 us
    pallas_call x1, Pallas kernels, on_device(): call(functools.partial(first_kernel, steps), (f32(width, width), f32(widt...  4.55 us
    unnamed x30, local copies, waits for them, and re-layouts  4.02 us
    pallas_call x1, Pallas kernels, on_device(): call(functools.partial(order_kernel, masks_a, masks_b, steps), (jax.Shape...  2.3 us
  transfers between devices with their start and end apart: 16, of which 7 were waited for; matrix products, arithmetic and copies ran while one was open for 4% of the time, Pallas kernels for 28%

commit v1 on v0

--- a/solution.py
+++ b/solution.py
@@ -95,6 +95,17 @@
     return lax.dot_general(
         a, b, (((0,), (0,)), ((), ())), precision=lax.Precision.HIGHEST, preferred_element_type=F32
     )
+
+
+def split3(x):
+    high, mid = split2(x)
+    return high, mid, (x - high.astype(F32) - mid.astype(F32)).astype(BF16)
+
+
+def stacked_at(a, b):
+    a_h, a_m, a_l = split3(a)
+    b_h, b_m, b_l = split3(b)
+    return mm_at(jnp.concatenate([a_h, a_h, a_m, a_m, a_h, a_l], 0), jnp.concatenate([b_h, b_m, b_h, b_m, b_l, b_h], 0))
 
 
 def lanes_below(count, rows, width):
@@ -164,15 +175,16 @@
     return rows
 
 
-def inverse_factor(work, beside=()):
+def inverse_factor(work, beside=(), start=0, stop=None):
     n = work.shape[0]
     beside = list(beside)
     slots = n // PANEL
-    for p in range(slots):
+    stop = slots if stop is None else stop
+    for p in range(start, stop):
         a = p * PANEL
         b = a + PANEL
         rows = [work[a + 8 * i : a + 8 * i + 8, :] for i in range(PANEL // 8)]
-        rows = factor_panel(rows, a, n, functools.partial(some_of, beside, n // 8))
+        rows = factor_panel(rows, a, n, functools.partial(some_of, beside, stop * PANEL // 8))
         for i in range(PANEL // 8):
             work[a + 8 * i : a + 8 * i + 8, :] = rows[i]
         if b < n:
@@ -181,12 +193,14 @@
             row = lax.broadcasted_iota(jnp.int32, (PANEL, n), 0)
             kept = jnp.where((lane > a + row) & (lane < b), 0.0, full)
             base = b // 128 * 128
-            update = exact_at(full[:, base:], kept)[b - base :]
+            update = stacked_at(full[:, base:], kept)[b - base :]
             lane = lax.broadcasted_iota(jnp.int32, (n - b, n), 1)
             rest = jnp.where((lane >= a) & (lane < b), 0.0, work[b:, :])
             work[b:, :] = rest - update
     while beside:
         beside.pop(0)()
+    if stop < slots:
+        return
     row = lax.broadcasted_iota(jnp.int32, (n, n), 0)
     lane = lax.broadcasted_iota(jnp.int32, (n, n), 1)
     work[...] = jnp.where(lane <= row, work[...], 0.0)
@@ -275,34 +289,31 @@
     return total
 
 
-def pieces_of(refs, which):
-    x, x1, x2, l3, r3 = refs
-    n, rows, width = l3.shape
-    return [r[...].reshape(n * rows, width) for r in (x.at[which], x1.at[which], x2.at[which], (l3, r3)[which])]
-
-
-def quarters(ref, k, width):
-    rows = ref.shape[0] // 4
-    return [ref[i * rows : (i + 1) * rows, k * width : (k + 1) * width] for i in range(4)]
-
-
-def middle_of(scal, step, steps, ar, b):
-    width = ar.shape[1] // steps
-    mid = summed(quarters(ar, step, width), pieces_of(b, 0))
+def pieces_of(refs):
+    return [r[...].reshape(r.shape[0] * r.shape[1], r.shape[2]) for r in refs]
+
+
+def split_rows(ref, count, at, width):
+    rows = ref.shape[0] // count
+    return [ref[i * rows : (i + 1) * rows, at : at + width] for i in range(count)]
+
+
+def masked(scal, step, steps, mid):
+    width = mid.shape[0]
     weight = scal[1 + 3 * steps + step].astype(F32)
     a_rank, b_rank = scal[1 + steps + step], scal[1 + 2 * steps + step]
     return mid * rows_below(a_rank, width, width) * lanes_below(b_rank, width, width) * weight
 
 
 def first_kernel(steps, scal, ar, probe, *refs):
-    b, (core, cross, mid_out, rp_out, k_out, y_out, gram_out) = refs[:5], refs[5:]
+    (x, x1, x2, l3, r3), (core, cross, mid_out, rp_out, k_out, y_out, gram_out) = refs[:5], refs[5:]
     width = mid_out.shape[0]
     tmask = lanes_below(scal[1], width, width)
     k_out[:width, :] = core[0] * rows_below(scal[0], width, width) * tmask
-    mid = middle_of(scal, 0, steps, ar, b)
+    b_left, b_right = pieces_of([x.at[0], x1.at[0], x2.at[0], l3]), pieces_of([x.at[1], x1.at[1], x2.at[1], r3])
+    mid = masked(scal, 0, steps, summed(split_rows(ar, 4, 0, width), b_left))
     mid_out[...] = mid
-    rows = probe.shape[0] // 4
-    rp = summed(pieces_of(b, 1), [probe[i * rows : (i + 1) * rows, :] for i in range(4)])
+    rp = summed(b_right, split_rows(probe, 4, 0, steps * width))
     rp_out[...] = rp[:, width:]
     k_out[width:, :] = exact(mid, rp[:, :width] * tmask)
     k = k_out[...]
@@ -311,85 +322,124 @@
     gram_out[...] = exact_at(k, y) + unit_beyond(scal[1], width)
 
 
-def inverse_kernel(tile, scal, gram, k0, y0, cross, mid0, rp01, core, w_out, core_out, h_out, t_v):
+def early_kernel(tile, scal, gram, k0, y0, cross, mid0, rp01, core, work_out, t_out):
     width = gram.shape[0]
     root = math.sqrt(tile)
-    w_out[...] = gram[...]
+    work_out[...] = gram[...]
 
     def next_core():
         y = jnp.concatenate([y0[:width, :] * rows_below(scal[0], width, width), y0[width:, :]], 0)
         z = jnp.concatenate([core[1], exact(mid0[...], rp01[...])], 0)
-        t_v[:, :width] = exact_at(y, z) * (1.0 / root)
+        t_out[:, :width] = exact_at(y, z) * (1.0 / root)
 
     def next_cross():
-        t_v[:, width:] = exact(cross[2 * width :, : 2 * width], k0[...]).T * root
-
-    inverse_factor(w_out, [next_core, next_cross])
-    both = exact(w_out[...], t_v[...])
+        t_out[:, width:] = exact(cross[2 * width :, : 2 * width], k0[...]).T * root
+
+    inverse_factor(work_out, [next_core, next_cross], 0, width // PANEL // 2)
+
+
+def late_kernel(masks_a, steps, scal, work, t, k0, y0, mid0, ar, probe, x, x1, x2, left, *refs):
+    n = len(masks_a)
+    al, (core_out, h_out, h_a_out, mid_out, rp_out, k_out, back_out, s_out) = refs[:n], refs[n : n + 8]
+    work_v, left_v, a_v, sems = refs[n + 8 :]
+    tile, width = left_v.shape
+    root = math.sqrt(tile)
+    late = place([r.at[:, 0] for r in al], masks_a, scal[1 + 4 * steps], a_v, sems, 0)
+    late.append(pltpu.make_async_copy(left, left_v, sems.at[n]))
+    work_v[...] = work[...]
+
+    def fetch():
+        for copy in late:
+            copy.start()
+
+    def middle_part():
+        mid_out[...] = summed(split_rows(ar, 4, width, width)[:3], pieces_of([r.at[0] for r in (x, x1, x2)]))
+
+    def probe_part():
+        rp_out[...] = summed(pieces_of([r.at[1] for r in (x, x1, x2)]), split_rows(probe, 4, width, width)[:3])
+
+    inverse_factor(work_v, [fetch, middle_part, probe_part], width // PANEL // 2)
+    w = work_v[...]
+    both = exact(w, t[...])
     keep = rows_below(scal[1], width, width)
-    core_out[...] = both[:, :width] * keep * lanes_below(scal[2], width, width)
-    h_out[...] = both[:, width:] * keep
+    a = both[:, :width] * keep * lanes_below(scal[2], width, width)
+    h = both[:, width:] * keep
+    core_out[...] = a
+    h_out[...] = h
+    h_a_out[...] = exact_at(h, a)
+    k_c = close(k0[...], close_at(w, a) * root)
+    k_out[...] = k_c
+    z = close_bt(y0[...], w)
+    back_out[:width, :] = z[:width] * rows_below(scal[0], width, width)
+    back_out[width:, :] = close_at(mid0[...], z[width:])
+    k_h, k_m = split2(k_c)
+    weights = jnp.concatenate([k_h[:width], k_h[:width], k_m[:width], k_h[width:], k_m[width:]], 0)
+    for copy in late:
+        copy.wait()
+    for c in range(tile // CHUNK):
+        at = slice(c * CHUNK, (c + 1) * CHUNK)
+        l_h, l_m = split2(left_v[at, :])
+        o = a_v[at, :]
+        s_out[at, :] = mm(jnp.concatenate([l_h, l_m, l_h, o, o], 1), weights)
 
 
 def second_kernel(
-    masks_a, masks_b, steps, scal, k0, y0, w0, core_c, h0, mid0, cross, ar, probe, *refs,
+    masks_a, masks_b, steps, scal, core_c, h0, h_a, mid_part, rp_part, k_c, back0, s_part, cross, ar, probe,
+    l3, r3, right, b0, b1, b2, br3, p0, p1, p2, pr3, *refs,
 ):
     n = len(masks_a)
-    b, refs = refs[:5], refs[5:]
-    left, right, b0, b1, b2, br3, p0, p1, p2, pr3 = refs[:10]
-    al, refs = refs[10 : 10 + n], refs[10 + n :]
-    out_left, out_right = refs[:2]
-    left_v, right_v, a_v, b_v, gram_v, k_v, q_v, outl_v, outr_v, sems, out_sems = refs[2:]
-    tile, width = left_v.shape
+    al, (out_left, out_right), refs = refs[:n], refs[n : n + 2], refs[n + 2 :]
+    right_v, a_v, b_v, gram_v, k_v, q_v, outl_v, outr_v, sems, out_sems = refs
+    tile, width = right_v.shape
     root = math.sqrt(tile)
     col_at, row_at = scal[1 + 4 * steps], scal[2 + 4 * steps]
-    late = []
-    for k, (x, x1, x2, r3) in enumerate(((p0, p1, p2, pr3), (b0, b1, b2, br3))):
+    late = place([r.at[:, 1] for r in al], masks_a, col_at, a_v, sems, 0)
+    for k, (x, x1, x2, x3) in enumerate(((p0, p1, p2, pr3), (b0, b1, b2, br3))):
         here = pl.ds(k * width, width)
-        late += place((x.at[1], x1.at[1], x2.at[1], r3), masks_b, row_at, b_v.at[:, here], sems, len(late))
-        late += place([r.at[:, k] for r in al], masks_a, col_at, a_v.at[:, here], sems, len(late))
-    late.append(pltpu.make_async_copy(left, left_v, sems.at[len(late)]))
+        late += place((x.at[1], x1.at[1], x2.at[1], x3), masks_b, row_at, b_v.at[:, here], sems, len(late))
     late.append(pltpu.make_async_copy(right, right_v, sems.at[len(late)]))
-    for copy in late:
-        copy.start()
     t0, t1 = scal[1], scal[2]
     a = core_c[...]
     h = h0[...]
-    h_a = exact_at(h, a)
-    mid1 = middle_of(scal, 1, steps, ar, b)
-    rp11 = summed(pieces_of(b, 1), quarters(probe, 1, width))
+    mid1 = masked(scal, 1, steps, mid_part[...] + summed(split_rows(ar, 4, width, width)[3:], pieces_of([l3])))
+    rp11 = rp_part[...] + summed(pieces_of([r3]), split_rows(probe, 4, width, width)[3:])
     core_b = exact(mid1, rp11 * lanes_below(t1, width, width))
     both = exact(jnp.concatenate([h, cross[2 * width :, 2 * width :]], 0), core_b)
     top = a * float(tile) + both[:width]
-    low = h_a + both[width:]
+    low = h_a[...] + both[width:]
     gram_v[...] = exact_at(jnp.concatenate([a, core_b], 0), jnp.concatenate([top, low], 0)) + unit_beyond(t1, width)
 
     def left_weights():
-        k_c = close(k0[...], close_at(w0[...], a) * root)
-        h, m = split2(jnp.concatenate([k_c, core_b], 0))
-        k_v[...] = jnp.concatenate([h[:width], h[:width], m[:width], h[width:], m[width:]], 0)
+        k_v[...] = jnp.concatenate(split2(core_b), 0)
 
     def right_weights():
-        z = close_bt(y0[...], w0[...])
-        back0 = jnp.concatenate([z[:width] * rows_below(scal[0], width, width), close_at(mid0[...], z[width:])], 0)
-        q_c = close(back0, top * rows_below(t0, width, width)) * (1.0 / tile)
+        q_c = close(back0[...], top * rows_below(t0, width, width)) * (1.0 / tile)
         h, m = split2(jnp.concatenate([q_c, close_at(mid1, low) * (1.0 / root)], 0))
         q_v[...] = jnp.concatenate([h[:width], h[:width], m[:width], h[width:], m[width:]], 0)
+
+    def fetch():
+        for copy in late:
+            copy.start()
 
     def arrive():
         for copy in late:
             copy.wait()
 
-    def form(out_v, factor, others, weights, c):
+    def form_left(c):
         at = slice(c * CHUNK, (c + 1) * CHUNK)
-        h, m = split2(factor[at, :])
-        o = others[at, :]
-        out_v[at, :] = mm(jnp.concatenate([h, m, h, o, o], 1), weights[...])
+        o = a_v[at, :]
+        outl_v[at, :] = s_part[at, :] + mm(jnp.concatenate([o, o], 1), k_v[...])
+
+    def form_right(c):
+        at = slice(c * CHUNK, (c + 1) * CHUNK)
+        h, m = split2(right_v[at, :])
+        o = b_v[at, :]
+        outr_v[at, :] = mm(jnp.concatenate([h, m, h, o, o], 1), q_v[...])
 
     count = tile // CHUNK
-    beside = [left_weights, right_weights, arrive]
-    beside += [functools.partial(form, outl_v, left_v, a_v, k_v, c) for c in range(count)]
-    beside += [functools.partial(form, outr_v, right_v, b_v, q_v, c) for c in range(count)]
+    beside = [fetch, left_weights, right_weights, arrive]
+    for form in (form_left, form_right):
+        beside += [functools.partial(form, c) for c in range(count)]
     inverse_factor(gram_v, beside)
     h, m = split2(gram_v[...])
     weights = jnp.concatenate([h, h, m], 1)
@@ -510,30 +560,43 @@
         20,
         20,
     )(scal, *ordered, *gathered[0], core, cross)
-    w0, core_c, h0 = call(
-        functools.partial(inverse_kernel, tile),
-        (f32(width, width),) * 3,
+    square = f32(width, width)
+    work, t = call(
+        functools.partial(early_kernel, tile),
+        (square, f32(width, 2 * width)),
         [sm] + [vm] * 7,
-        [VMEM((width, 2 * width), F32)],
-        "inverse_factor",
+        [],
+        "factor_early",
+        20,
+        15,
+    )(scal, gram, k0, y0, cross, mid0, rp01, core)
+    x, x1, x2, l3, r3 = gathered[1]
+    tall = f32(2 * width, width)
+    state = call(
+        functools.partial(late_kernel, masks_a, steps),
+        (square, square, square, square, square, tall, tall, f32(tile, width)),
+        [sm] + [vm] * 10 + [any_] * (1 + cols_count),
+        [VMEM((width, width), F32), whole, VMEM((tile, width), BF16), dma((cols_count + 1,))],
+        "factor_late",
         24,
-        30,
-    )(scal, gram, k0, y0, cross, mid0, rp01, core)
-    weights = VMEM(((3 + 2 * steps) * width, width), BF16)
-    late_b = [g[i] for g in (gathered[1], gathered[0]) for i in (0, 1, 2, 4)]
+        25,
+    )(scal, work, t, k0, y0, mid0, *ordered, x, x1, x2, left, *al)
     out_left, out_right = call(
         functools.partial(second_kernel, masks_a, masks_b, steps),
         (f32(tile, width), f32(tile, width)),
-        [sm] + [vm] * 14 + [any_] * (10 + cols_count),
+        [sm] + [vm] * 13 + [any_] * (9 + cols_count),
         [
-            whole, whole, wide, wide, VMEM((width, width), F32), weights, weights, whole, whole,
-            dma((2 * rows_count + steps * cols_count + 2,)), dma((2 * (tile // CHUNK),)),
+            whole, VMEM((tile, width), BF16), wide, VMEM((width, width), F32),
+            VMEM((2 * width, width), BF16), VMEM(((3 + 2 * steps) * width, width), BF16), whole, whole,
+            dma((2 * rows_count + cols_count + 1,)), dma((2 * (tile // CHUNK),)),
         ],
         "second_step",
         36,
         100,
         ANY,
-    )(scal, k0, y0, w0, core_c, h0, mid0, cross, *ordered, *gathered[1], left, right, *late_b, *al)
+    )(
+        scal, *state, cross, *ordered, l3, r3, right, x, x1, x2, r3, *[gathered[0][i] for i in (0, 1, 2, 4)], *al
+    )
     return (out_left[None, None], out_right[None, None])
 
 

time: 85.6 us -> 81.3 us (0.950)
  waiting for transfers between devices: 14.6 us -> 9.55 us
  Pallas kernels: 42.4 us -> 43.4 us
    ppermute x16, waiting for transfers between devices: 14.6 us -> 9.55 us  [exchange(): return lax.ppermute(x, axis, [(r, r ^ bit) for r in range(size)])]
    pallas_call x1 -> x2, Pallas kernels: 9.76 us -> 13.4 us  [the longest x1 8.46 us: on_device(): call(functools.partial(late_kernel, masks_a, steps), (square, square, squ...]
    pallas_call x1, Pallas kernels: 18.6 us -> 16 us  [on_device(): call(functools.partial(second_kernel, masks_a, masks_b, steps), (f32(tile...]
  transfers between devices with their start and end apart: 16 -> 16, of which waited for: 7 -> 5; matrix products, arithmetic and copies ran while one was open for 4% -> 4% of each run, Pallas kernels for 28% -> 34%
where the time goes in v1:
time: 81.3 us; the launch traced here: 80.9 us
  Pallas kernels  43.4 us (53%)
  starting transfers between devices  18.7 us (23%)
  waiting for transfers between devices  9.55 us (12%)
  local copies, waits for them, and re-layouts  5.79 us (7%)
  between operations  1.78 us (2%)
  other arithmetic  1.7 us (2%)
    ppermute x16, starting transfers between devices, exchange(): return lax.ppermute(x, axis, [(r, r ^ bit) for r in range(size)])  18.7 us
    pallas_call x1, Pallas kernels, on_device(): call(functools.partial(second_kernel, masks_a, masks_b, steps), (f32(tile...  16 us
    ppermute x16, waiting for transfers between devices, exchange(): return lax.ppermute(x, axis, [(r, r ^ bit) for r in range(size)])  9.55 us
    pallas_call x1, Pallas kernels, on_device(): call(functools.partial(late_kernel, masks_a, steps), (square, square, squ...  8.46 us
    pallas_call x1, Pallas kernels, on_device(): call(functools.partial(cross_kernel, masks_a, steps), f32((1 + steps) * w...  5.53 us
    pallas_call x1, Pallas kernels, on_device(): call(functools.partial(early_kernel, tile), (square, f32(width, 2 * width...  4.95 us
    pallas_call x1, Pallas kernels, on_device(): call(functools.partial(first_kernel, steps), (f32(width, width), f32(widt...  4.55 us
    unnamed x30, local copies, waits for them, and re-layouts  4.02 us
  transfers between devices with their start and end apart: 16, of which 5 were waited for; matrix products, arithmetic and copies ran while one was open for 4% of the time, Pallas kernels for 34%

profile of v1, /device:TPU:0, one launch (start us, length us, event | category | flops | bytes accessed | tf_op | source)
XLA Modules:
  0.0 80.9 jit_solution(4330326596859323880)
XLA Ops:
  0.6 0.5 collective-permute-start.4
  1.2 1.0 %slice_bitcast_fusion.4 = (bf16[1,128,256]{2,1,0:T(8,128)(2,1)S(1)}, bf16[1,128,256]{2,1,0:T(8,128)(2,1)S(1)}, bf16[1,128,256]{2,1,0:T(8,128)(2,1)S(1)}, bf16[1,128,256]{2,1,0:T(8,128)(2,1)S(1)}) fusion(bf16[2,1,128,256]{3,2,1,0:T(8,128)(2,1)} %param.21, bf16[2,1,128,256]{3,2,1,0:T(8,128)(2,1)} %param.20), kind=kLoop, calls=%fused_computation.8 | loop fusion | bytes 524288 | tf_op jit(solution)/shard_map/stack;squeeze | solution.py:526
  2.1 2.7 %collective-permute-start.2 = (bf16[2,1,128,256]{3,2,1,0:T(8,128)(2,1)S(1)}, bf16[2,1,128,256]{3,2,1,0:T(8,128)(2,1)S(1)}, u32[]{:S(2)}, u32[]{:S(2)}) collective-permute-start(bf16[2,1,128,256]{3,2,1,0:T(8,128)(2,1)S(1)} %maximum_bitcast_fusion), channel_id=1, source_target_pairs={{0,8},{2,10},{4,12},{6,14},{8,0},{10,2},{12,4},{14,6},{16,24},{18,... | collective-permute-start | bytes 393224 | tf_op jit(solution)/shard_map/ppermute | solution.py:21
  4.8 2.6 %collective-permute-start.1 = (bf16[2,1,128,256]{3,2,1,0:T(8,128)(2,1)S(1)}, bf16[2,1,128,256]{3,2,1,0:T(8,128)(2,1)}, u32[]{:S(2)}, u32[]{:S(2)}) collective-permute-start(bf16[2,1,128,256]{3,2,1,0:T(8,128)(2,1)S(1)} %maximum_bitcast_fusion), channel_id=1, source_target_pairs={{0,16},{2,18},{4,20},{6,22},{8,24},{10,26},{12,28},{14,30},{16,0},... | collective-permute-start | bytes 393224 | tf_op jit(solution)/shard_map/ppermute | solution.py:21
  7.4 1.6 %copy-done = bf16[2,2048,256]{2,1,0:T(8,128)(2,1)S(1)} copy-done((bf16[2,2048,256]{2,1,0:T(8,128)(2,1)S(1)}, bf16[2,2048,256]{2,1,0:T(8,128)(2,1)}, u32[]{:S(2)}) %copy-start) | copy-done | bytes 2097176
  9.0 1.6 %copy-done.3 = f32[1,1,2048,256]{3,2,1,0:T(8,128)S(1)} copy-done((f32[1,1,2048,256]{3,2,1,0:T(8,128)S(1)}, f32[1,1,2048,256]{3,2,1,0:T(8,128)}, u32[]{:S(2)}) %copy-start.3) | copy-done | bytes 2097176
  10.6 0.0 copy-start.12
  10.6 0.0 copy-start.2
  10.6 0.0 copy-start.6
  10.6 1.6 %right_probe.1.refs_5_.core = f32[2,256,256]{2,1,0:T(8,128)S(1)} custom-call(f32[2048,256]{1,0:T(8,128)S(1)} %bitcast.37, bf16[2,2048,256]{2,1,0:T(8,128)(2,1)S(1)} %copy-done), custom_call_target="tpu_custom_call" | custom-call | flops 3221225472 | bytes 1048576 | tf_op jit(solution)/shard_map/right_probe/pallas_call | solution.py:506
  12.2 0.0 copy-start.8
  12.3 0.8 copy-done.8
  13.0 1.2 %collective-permute-done.1 = bf16[2,1,128,256]{3,2,1,0:T(8,128)(2,1)} collective-permute-done((bf16[2,1,128,256]{3,2,1,0:T(8,128)(2,1)S(1)}, bf16[2,1,128,256]{3,2,1,0:T(8,128)(2,1)}, u32[]{:S(2)}, u32[]{:S(2)}) %collective-permute-start.1) | collective-permute-done | bytes 131104 | tf_op jit(solution)/shard_map/ppermute | solution.py:21
  14.3 0.4 collective-permute-start.3
  14.7 0.6 bitcast_multiply_fusion
  16.0 0.7 concatenate.9.scal
  16.7 0.0 collective-permute-done.2
  16.7 2.8 %collective-permute-done.3 = bf16[2,1,128,256]{3,2,1,0:T(8,128)(2,1)} collective-permute-done((bf16[2,1,128,256]{3,2,1,0:T(8,128)(2,1)}, bf16[2,1,128,256]{3,2,1,0:T(8,128)(2,1)}, u32[]{:S(2)}, u32[]{:S(2)}) %collective-permute-start.3) | collective-permute-done | bytes 131104 | tf_op jit(solution)/shard_map/ppermute | solution.py:21
  19.5 1.0 %pad_maximum_fusion.refs_0_.p0 = bf16[2,4,128,256]{3,2,1,0:T(8,128)(2,1)S(1)} fusion(bf16[2,1,128,256]{3,2,1,0:T(8,128)(2,1)} %collective-permute-done.3, bf16[2,1,128,256]{3,2,1,0:T(8,128)(2,1)S(1)} %collective-permute-done.2, bf16[2,1,128,256]{3,2,1,0:T(8,128)(2,1)} %collective-permute-done.1, bf16[2,1,128,256]{3,2,1,0:T(8,128)(2,1)S(1)} %maximum_bitcast_fusion), kind=kLoop, calls=%fused_computation | loop fusion | flops 786432 | bytes 1048576 | tf_op jit(solution)/shard_map/concatenate | solution.py:542
  20.6 1.6 %collective-permute-start.6 = (bf16[2,4,128,256]{3,2,1,0:T(8,128)(2,1)S(1)}, bf16[2,4,128,256]{3,2,1,0:T(8,128)(2,1)S(1)}, u32[]{:S(2)}, u32[]{:S(2)}) collective-permute-start(bf16[2,4,128,256]{3,2,1,0:T(8,128)(2,1)S(1)} %pad_maximum_fusion.refs_0_.p0), channel_id=1, source_target_pairs={{0,4},{2,6},{4,0},{6,2},{8,12},{10,14},{12,8},{14,10},{16,20},{18,... | collective-permute-start | bytes 1572872 | tf_op jit(solution)/shard_map/ppermute | solution.py:21
  22.2 1.5 %collective-permute-start.5 = (bf16[2,4,128,256]{3,2,1,0:T(8,128)(2,1)S(1)}, bf16[2,4,128,256]{3,2,1,0:T(8,128)(2,1)S(1)}, u32[]{:S(2)}, u32[]{:S(2)}) collective-permute-start(bf16[2,4,128,256]{3,2,1,0:T(8,128)(2,1)S(1)} %pad_maximum_fusion.refs_0_.p0), channel_id=1, source_target_pairs={{0,2},{2,0},{4,6},{6,4},{8,10},{10,8},{12,14},{14,12},{16,18},{18,... | collective-permute-start | bytes 1572872 | tf_op jit(solution)/shard_map/ppermute | solution.py:21
  23.7 1.1 %collective-permute-start.9 = (bf16[2,1,128,256]{3,2,1,0:T(8,128)(2,1)S(1)}, bf16[2,1,128,256]{3,2,1,0:T(8,128)(2,1)S(1)}, u32[]{:S(2)}, u32[]{:S(2)}) collective-permute-start(bf16[2,1,128,256]{3,2,1,0:T(8,128)(2,1)S(1)} %maximum_bitcast_fusion.1), channel_id=1, source_target_pairs={{0,16},{2,18},{4,20},{6,22},{8,24},{10,26},{12,28},{14,30},{16,0},... | collective-permute-start | bytes 393224 | tf_op jit(solution)/shard_map/ppermute | solution.py:21
  24.8 5.5 %left_cross.1.refs_6_.cross = f32[768,768]{1,0:T(8,128)S(1)} custom-call(s32[11]{0:T(128)S(1)} %concatenate.9.scal, f32[2048,256]{1,0:T(8,128)S(1)} %bitcast.35, bf16[1,2,1024,256]{3,2,1,0:T(8,128)(2,1)S(1)} %copy-done.6, bf16[1,2,1024,256]{3,2,1,0:T(8,128)(2,1)} %collective-permute-done.4.refs_1_), custom_call_target="tpu_custom_call" | custom-call | flops 6442450944 | bytes 1048576 | tf_op jit(solution)/shard_map/left_cross/pallas_call | solution.py:515
  30.3 0.0 collective-permute-done.refs_1_
  30.4 2.3 %ordered.1 = (bf16[2048,512]{1,0:T(8,128)(2,1)S(1)}, bf16[2048,512]{1,0:T(8,128)(2,1)S(1)}) custom-call(s32[11]{0:T(128)S(1)} %concatenate.9.scal, bf16[2,2048,256]{2,1,0:T(8,128)(2,1)S(1)} %copy-done.1, bf16[1,2,1024,256]{3,2,1,0:T(8,128)(2,1)S(1)} %copy-done.5, bf16[1,2,1024,256]{3,2,1,0:T(8,128)(2,1)} %collective-permute-done.refs_1_), custom_call_target="tpu_custom_call" | custom-call | flops 1342177280 | bytes 1048576 | tf_op jit(solution)/shard_map/ordered/pallas_call | solution.py:531
  32.7 0.0 copy-start.9
  32.7 0.0 collective-permute-done.6.refs_2_.p2
  32.7 1.1 %collective-permute-done.5.refs_1_.p1 = bf16[2,4,128,256]{3,2,1,0:T(8,128)(2,1)S(1)} collective-permute-done((bf16[2,4,128,256]{3,2,1,0:T(8,128)(2,1)S(1)}, bf16[2,4,128,256]{3,2,1,0:T(8,128)(2,1)S(1)}, u32[]{:S(2)}, u32[]{:S(2)}) %collective-permute-start.5) | collective-permute-done | bytes 524320 | tf_op jit(solution)/shard_map/ppermute | solution.py:21
  33.9 0.6 collective-permute-start.7
  34.5 1.5 %collective-permute-start.8 = (bf16[4,128,256]{2,1,0:T(8,128)(2,1)S(1)}, bf16[4,128,256]{2,1,0:T(8,128)(2,1)S(1)}, u32[]{:S(2)}, u32[]{:S(2)}) collective-permute-start(bf16[4,128,256]{2,1,0:T(8,128)(2,1)S(1)} %slice_bitcast_fusion.2), channel_id=1, source_target_pairs={{0,2},{2,0},{4,6},{6,4},{8,10},{10,8},{12,14},{14,12},{16,18},{18,... | collective-permute-start | bytes 786440 | tf_op jit(solution)/shard_map/ppermute | solution.py:21
  36.0 1.1 %collective-permute-start.10 = (bf16[2,1,128,256]{3,2,1,0:T(8,128)(2,1)S(1)}, bf16[2,1,128,256]{3,2,1,0:T(8,128)(2,1)S(1)}, u32[]{:S(2)}, u32[]{:S(2)}) collective-permute-start(bf16[2,1,128,256]{3,2,1,0:T(8,128)(2,1)S(1)} %maximum_bitcast_fusion.1), channel_id=1, source_target_pairs={{0,8},{2,10},{4,12},{6,14},{8,0},{10,2},{12,4},{14,6},{16,24},{18,... | collective-permute-start | bytes 393224 | tf_op jit(solution)/shard_map/ppermute | solution.py:21
  37.1 0.0 collective-permute-done.9
  37.1 0.9 %collective-permute-start.11 = (bf16[2,1,128,256]{3,2,1,0:T(8,128)(2,1)S(1)}, bf16[2,1,128,256]{3,2,1,0:T(8,128)(2,1)S(1)}, u32[]{:S(2)}, u32[]{:S(2)}) collective-permute-start(bf16[2,1,128,256]{3,2,1,0:T(8,128)(2,1)S(1)} %collective-permute-done.9), channel_id=1, source_target_pairs={{0,8},{2,10},{4,12},{6,14},{8,0},{10,2},{12,4},{14,6},{16,24},{18,... | collective-permute-start | bytes 393224 | tf_op jit(solution)/shard_map/ppermute | solution.py:21
  38.0 2.9 %collective-permute-done.10 = bf16[2,1,128,256]{3,2,1,0:T(8,128)(2,1)S(1)} collective-permute-done((bf16[2,1,128,256]{3,2,1,0:T(8,128)(2,1)S(1)}, bf16[2,1,128,256]{3,2,1,0:T(8,128)(2,1)S(1)}, u32[]{:S(2)}, u32[]{:S(2)}) %collective-permute-start.10) | collective-permute-done | bytes 131104 | tf_op jit(solution)/shard_map/ppermute | solution.py:21
  40.9 1.4 %collective-permute-done.11 = bf16[2,1,128,256]{3,2,1,0:T(8,128)(2,1)S(1)} collective-permute-done((bf16[2,1,128,256]{3,2,1,0:T(8,128)(2,1)S(1)}, bf16[2,1,128,256]{3,2,1,0:T(8,128)(2,1)S(1)}, u32[]{:S(2)}, u32[]{:S(2)}) %collective-permute-start.11) | collective-permute-done | bytes 131104 | tf_op jit(solution)/shard_map/ppermute | solution.py:21
  42.3 0.1 pad_maximum_fusion.1.x.b0
  42.4 0.0 collective-permute-done.8.refs_4_.pr3
  42.4 1.6 %collective-permute-start.13 = (bf16[2,4,128,256]{3,2,1,0:T(8,128)(2,1)S(1)}, bf16[2,4,128,256]{3,2,1,0:T(8,128)(2,1)S(1)}, u32[]{:S(2)}, u32[]{:S(2)}) collective-permute-start(bf16[2,4,128,256]{3,2,1,0:T(8,128)(2,1)S(1)} %pad_maximum_fusion.1.x.b0), channel_id=1, source_target_pairs={{0,4},{2,6},{4,0},{6,2},{8,12},{10,14},{12,8},{14,10},{16,20},{18,... | collective-permute-start | bytes 1572872 | tf_op jit(solution)/shard_map/ppermute | solution.py:21
  44.0 0.8 collective-permute-start.12
  44.8 4.5 %first_step.1 = (f32[256,256]{1,0:T(8,128)S(1)}, f32[256,256]{1,0:T(8,128)S(1)}, f32[512,256]{1,0:T(8,128)S(1)}, f32[512,256]{1,0:T(8,128)S(1)}, f32[256,256]{1,0:T(8,128)S(1)}) custom-call(s32[11]{0:T(128)S(1)} %concatenate.9.scal, bf16[2048,512]{1,0:T(8,128)(2,1)S(1)} %get-tuple-element.26.ar, bf16[2048,512]{1,0:T(8,128)(2,1)S(1)} %get-tuple-element.27.probe, ...), custom_call_target="tpu_custom_call" | custom-call | flops 5368709120 | bytes 1048576 | tf_op jit(solution)/shard_map/first_step/pallas_call | solution.py:554
  49.4 4.9 %factor_early.1 = (f32[256,256]{1,0:T(8,128)S(1)}, f32[256,512]{1,0:T(8,128)S(1)}) custom-call(s32[11]{0:T(128)S(1)} %concatenate.9.scal, f32[256,256]{1,0:T(8,128)S(1)} %get-tuple-element.31.gram, f32[512,256]{1,0:T(8,128)S(1)} %get-tuple-element.32.k0, f32[512,256]{1,0:T(8,128)S(1)} %get-tuple-element.33.y0, f32[768,768]{1,0:T(8,128)S(1)} %left_cross.1.refs_6_.cross, ...), custom_call_target="tpu_custom_call" | custom-call | flops 4026531840 | bytes 1048576 | tf_op jit(solution)/shard_map/factor_early/pallas_call | solution.py:564
  54.4 1.3 %collective-permute-start.15 = (bf16[4,128,256]{2,1,0:T(8,128)(2,1)S(1)}, bf16[4,128,256]{2,1,0:T(8,128)(2,1)S(1)}, u32[]{:S(2)}, u32[]{:S(2)}) collective-permute-start(bf16[4,128,256]{2,1,0:T(8,128)(2,1)S(1)} %slice_bitcast_fusion), channel_id=1, source_target_pairs={{0,2},{2,0},{4,6},{6,4},{8,10},{10,8},{12,14},{14,12},{16,18},{18,... | collective-permute-start | bytes 786440 | tf_op jit(solution)/shard_map/ppermute | solution.py:21
  55.7 0.0 collective-permute-done.12.x1.b1
  55.7 0.6 collective-permute-start.14
  56.3 8.5 %factor_late.1 = (f32[256,256]{1,0:T(8,128)S(1)}, f32[256,256]{1,0:T(8,128)S(1)}, f32[256,256]{1,0:T(8,128)S(1)}, f32[256,256]{1,0:T(8,128)S(1)}, f32[256,256]{1...) custom-call(s32[11]{0:T(128)S(1)} %concatenate.9.scal, ...), custom_call_target="tpu_custom_call" | custom-call | flops 6710886400 | bytes 1048576 | tf_op jit(solution)/shard_map/factor_late/pallas_call | solution.py:575
  64.7 0.0 collective-permute-done.15.r3.br3
  64.7 0.0 collective-permute-done.14.l3
  64.8 16.0 %second_step.1 = (f32[2048,256]{1,0:T(8,128)}, f32[2048,256]{1,0:T(8,128)}) custom-call(s32[11]{0:T(128)S(1)} %concatenate.9.scal, f32[256,256]{1,0:T(8,128)S(1)} %get-tuple-element.40.core_c, f32[256,256]{1,0:T(8,128)S(1)} %get-tuple-element.41.h0, f32[256,256]{1,0:T(8,128)S(1)} %get-tuple-element.42.h_a, f32[256,256]{1,0:T(8,128)S(1)} %get-tuple-element.43.mid_part, ...), custom_call_target="tpu_custom_call" | custom-call | flops 26843545600 | bytes 1048576 | tf_op jit(solution)/shard_map/second_step/pallas_call | solution.py:584
  (32 shorter events, 0.2 us)
Async XLA Ops:
  0.6 20.0 %collective-permute-start.4 = (bf16[1,2,1024,256]{3,2,1,0:T(8,128)(2,1)}, bf16[1,2,1024,256]{3,2,1,0:T(8,128)(2,1)}, u32[]{:S(2)}, u32[]{:S(2)}) collective-permute-start(bf16[1,2,1024,256]{3,2,1,0:T(8,128)(2,1)} %refs_0_.7), channel_id=1, source_target_pairs={{0,1},{1,0},{2,3},{3,2},{4,5},{5,4},{6,7},{7,6},{8,9},{9,8},{10,11... | collective-permute-start | bytes 3145736 | tf_op jit(solution)/shard_map/ppermute | solution.py:21
  2.1 14.6 %collective-permute-start.2 = (bf16[2,1,128,256]{3,2,1,0:T(8,128)(2,1)S(1)}, bf16[2,1,128,256]{3,2,1,0:T(8,128)(2,1)S(1)}, u32[]{:S(2)}, u32[]{:S(2)}) collective-permute-start(bf16[2,1,128,256]{3,2,1,0:T(8,128)(2,1)S(1)} %maximum_bitcast_fusion), channel_id=1, source_target_pairs={{0,8},{2,10},{4,12},{6,14},{8,0},{10,2},{12,4},{14,6},{16,24},{18,... | collective-permute-start | bytes 393224 | tf_op jit(solution)/shard_map/ppermute | solution.py:21
  4.8 9.5 %collective-permute-start.1 = (bf16[2,1,128,256]{3,2,1,0:T(8,128)(2,1)S(1)}, bf16[2,1,128,256]{3,2,1,0:T(8,128)(2,1)}, u32[]{:S(2)}, u32[]{:S(2)}) collective-permute-start(bf16[2,1,128,256]{3,2,1,0:T(8,128)(2,1)S(1)} %maximum_bitcast_fusion), channel_id=1, source_target_pairs={{0,16},{2,18},{4,20},{6,22},{8,24},{10,26},{12,28},{14,30},{16,0},... | collective-permute-start | bytes 393224 | tf_op jit(solution)/shard_map/ppermute | solution.py:21
  7.4 23.0 %collective-permute-start = (bf16[1,2,1024,256]{3,2,1,0:T(8,128)(2,1)}, bf16[1,2,1024,256]{3,2,1,0:T(8,128)(2,1)}, u32[]{:S(2)}, u32[]{:S(2)}) collective-permute-start(bf16[1,2,1024,256]{3,2,1,0:T(8,128)(2,1)} %refs_0_.4), channel_id=1, source_target_pairs={{0,1},{1,0},{2,3},{3,2},{4,5},{5,4},{6,7},{7,6},{8,9},{9,8},{10,11... | collective-permute-start | bytes 3145736 | tf_op jit(solution)/shard_map/ppermute | solution.py:21
  7.4 1.6 %copy-start = (bf16[2,2048,256]{2,1,0:T(8,128)(2,1)S(1)}, bf16[2,2048,256]{2,1,0:T(8,128)(2,1)}, u32[]{:S(2)}) copy-start(bf16[2,2048,256]{2,1,0:T(8,128)(2,1)} %probe.3) | copy-start | bytes 6291460
  9.0 1.6 %copy-start.3 = (f32[1,1,2048,256]{3,2,1,0:T(8,128)S(1)}, f32[1,1,2048,256]{3,2,1,0:T(8,128)}, u32[]{:S(2)}) copy-start(f32[1,1,2048,256]{3,2,1,0:T(8,128)} %param.14) | copy-start | bytes 6291460
  10.6 4.1 %copy-start.13 = (s32[2,1]{0,1:T(1,128)S(1)}, s32[2,1]{0,1:T(1,128)}, u32[]{:S(2)}) copy-start(s32[2,1]{0,1:T(1,128)} %param.23) | copy-start | bytes 28
  10.6 4.1 %copy-start.14 = (s32[1,2]{1,0:T(1,128)S(1)}, s32[1,2]{1,0:T(1,128)}, u32[]{:S(2)}) copy-start(s32[1,2]{1,0:T(1,128)} %param.19) | copy-start | bytes 28
  10.6 5.4 %copy-start.10 = (s32[1,1,2]{2,1,0:T(1,128)S(1)}, s32[1,1,2]{2,1,0:T(1,128)}, u32[]{:S(2)}) copy-start(s32[1,1,2]{2,1,0:T(1,128)} %param.25) | copy-start | bytes 28
  10.6 5.4 %copy-start.11 = (s32[1,2]{1,0:T(1,128)S(1)}, s32[1,2]{1,0:T(1,128)}, u32[]{:S(2)}) copy-start(s32[1,2]{1,0:T(1,128)} %param.18) | copy-start | bytes 28
  10.6 5.4 %copy-start.12 = (s32[2,1]{0,1:T(1,128)S(1)}, s32[2,1]{0,1:T(1,128)}, u32[]{:S(2)}) copy-start(s32[2,1]{0,1:T(1,128)} %param.22) | copy-start | bytes 28
  10.6 14.2 %copy-start.2 = (f32[1,1,2048,256]{3,2,1,0:T(8,128)S(1)}, f32[1,1,2048,256]{3,2,1,0:T(8,128)}, u32[]{:S(2)}) copy-start(f32[1,1,2048,256]{3,2,1,0:T(8,128)} %param.13) | copy-start | bytes 6291460
  10.6 14.2 %copy-start.6 = (bf16[1,2,1024,256]{3,2,1,0:T(8,128)(2,1)S(1)}, bf16[1,2,1024,256]{3,2,1,0:T(8,128)(2,1)}, u32[]{:S(2)}) copy-start(bf16[1,2,1024,256]{3,2,1,0:T(8,128)(2,1)} %refs_0_.7) | copy-start | bytes 3145732
  12.2 0.8 copy-start.8
  14.3 5.3 %collective-permute-start.3 = (bf16[2,1,128,256]{3,2,1,0:T(8,128)(2,1)}, bf16[2,1,128,256]{3,2,1,0:T(8,128)(2,1)}, u32[]{:S(2)}, u32[]{:S(2)}) collective-permute-start(bf16[2,1,128,256]{3,2,1,0:T(8,128)(2,1)} %collective-permute-done.1), channel_id=1, source_target_pairs={{0,8},{2,10},{4,12},{6,14},{8,0},{10,2},{12,4},{14,6},{16,24},{18,... | collective-permute-start | bytes 393224 | tf_op jit(solution)/shard_map/ppermute | solution.py:21
  20.6 12.1 %collective-permute-start.6 = (bf16[2,4,128,256]{3,2,1,0:T(8,128)(2,1)S(1)}, bf16[2,4,128,256]{3,2,1,0:T(8,128)(2,1)S(1)}, u32[]{:S(2)}, u32[]{:S(2)}) collective-permute-start(bf16[2,4,128,256]{3,2,1,0:T(8,128)(2,1)S(1)} %pad_maximum_fusion.refs_0_.p0), channel_id=1, source_target_pairs={{0,4},{2,6},{4,0},{6,2},{8,12},{10,14},{12,8},{14,10},{16,20},{18,... | collective-permute-start | bytes 1572872 | tf_op jit(solution)/shard_map/ppermute | solution.py:21
  22.2 11.7 %collective-permute-start.5 = (bf16[2,4,128,256]{3,2,1,0:T(8,128)(2,1)S(1)}, bf16[2,4,128,256]{3,2,1,0:T(8,128)(2,1)S(1)}, u32[]{:S(2)}, u32[]{:S(2)}) collective-permute-start(bf16[2,4,128,256]{3,2,1,0:T(8,128)(2,1)S(1)} %pad_maximum_fusion.refs_0_.p0), channel_id=1, source_target_pairs={{0,2},{2,0},{4,6},{6,4},{8,10},{10,8},{12,14},{14,12},{16,18},{18,... | collective-permute-start | bytes 1572872 | tf_op jit(solution)/shard_map/ppermute | solution.py:21
  23.7 13.4 %collective-permute-start.9 = (bf16[2,1,128,256]{3,2,1,0:T(8,128)(2,1)S(1)}, bf16[2,1,128,256]{3,2,1,0:T(8,128)(2,1)S(1)}, u32[]{:S(2)}, u32[]{:S(2)}) collective-permute-start(bf16[2,1,128,256]{3,2,1,0:T(8,128)(2,1)S(1)} %maximum_bitcast_fusion.1), channel_id=1, source_target_pairs={{0,16},{2,18},{4,20},{6,22},{8,24},{10,26},{12,28},{14,30},{16,0},... | collective-permute-start | bytes 393224 | tf_op jit(solution)/shard_map/ppermute | solution.py:21
  24.8 5.6 %copy-start.1 = (bf16[2,2048,256]{2,1,0:T(8,128)(2,1)S(1)}, bf16[2,2048,256]{2,1,0:T(8,128)(2,1)}, u32[]{:S(2)}) copy-start(bf16[2,2048,256]{2,1,0:T(8,128)(2,1)} %probe.3) | copy-start | bytes 6291460
  24.8 5.6 %copy-start.5 = (bf16[1,2,1024,256]{3,2,1,0:T(8,128)(2,1)S(1)}, bf16[1,2,1024,256]{3,2,1,0:T(8,128)(2,1)}, u32[]{:S(2)}) copy-start(bf16[1,2,1024,256]{3,2,1,0:T(8,128)(2,1)} %refs_0_.4) | copy-start | bytes 3145732
  30.3 19.0 %copy-start.7 = (f32[768,768]{1,0:T(8,128)}, f32[768,768]{1,0:T(8,128)S(1)}, u32[]{:S(2)}) copy-start(f32[768,768]{1,0:T(8,128)S(1)} %left_cross.1.refs_6_.cross) | copy-start | bytes 7077892
  32.7 12.1 %copy-start.9 = (f32[2,256,256]{2,1,0:T(8,128)S(1)}, f32[2,256,256]{2,1,0:T(8,128)}, u32[]{:S(2)}) copy-start(f32[2,256,256]{2,1,0:T(8,128)} %copy-done.8) | copy-start | bytes 1572868
  33.9 8.5 %collective-permute-start.7 = (bf16[4,128,256]{2,1,0:T(8,128)(2,1)S(1)}, bf16[4,128,256]{2,1,0:T(8,128)(2,1)S(1)}, u32[]{:S(2)}, u32[]{:S(2)}) collective-permute-start(bf16[4,128,256]{2,1,0:T(8,128)(2,1)S(1)} %slice_bitcast_fusion.3), channel_id=1, source_target_pairs={{0,4},{2,6},{4,0},{6,2},{8,12},{10,14},{12,8},{14,10},{16,20},{18,... | collective-permute-start | bytes 786440 | tf_op jit(solution)/shard_map/ppermute | solution.py:21
  34.5 7.9 %collective-permute-start.8 = (bf16[4,128,256]{2,1,0:T(8,128)(2,1)S(1)}, bf16[4,128,256]{2,1,0:T(8,128)(2,1)S(1)}, u32[]{:S(2)}, u32[]{:S(2)}) collective-permute-start(bf16[4,128,256]{2,1,0:T(8,128)(2,1)S(1)} %slice_bitcast_fusion.2), channel_id=1, source_target_pairs={{0,2},{2,0},{4,6},{6,4},{8,10},{10,8},{12,14},{14,12},{16,18},{18,... | collective-permute-start | bytes 786440 | tf_op jit(solution)/shard_map/ppermute | solution.py:21
  36.0 5.0 %collective-permute-start.10 = (bf16[2,1,128,256]{3,2,1,0:T(8,128)(2,1)S(1)}, bf16[2,1,128,256]{3,2,1,0:T(8,128)(2,1)S(1)}, u32[]{:S(2)}, u32[]{:S(2)}) collective-permute-start(bf16[2,1,128,256]{3,2,1,0:T(8,128)(2,1)S(1)} %maximum_bitcast_fusion.1), channel_id=1, source_target_pairs={{0,8},{2,10},{4,12},{6,14},{8,0},{10,2},{12,4},{14,6},{16,24},{18,... | collective-permute-start | bytes 393224 | tf_op jit(solution)/shard_map/ppermute | solution.py:21
  37.1 5.2 %collective-permute-start.11 = (bf16[2,1,128,256]{3,2,1,0:T(8,128)(2,1)S(1)}, bf16[2,1,128,256]{3,2,1,0:T(8,128)(2,1)S(1)}, u32[]{:S(2)}, u32[]{:S(2)}) collective-permute-start(bf16[2,1,128,256]{3,2,1,0:T(8,128)(2,1)S(1)} %collective-permute-done.9), channel_id=1, source_target_pairs={{0,8},{2,10},{4,12},{6,14},{8,0},{10,2},{12,4},{14,6},{16,24},{18,... | collective-permute-start | bytes 393224 | tf_op jit(solution)/shard_map/ppermute | solution.py:21
  42.4 11.9 %collective-permute-start.13 = (bf16[2,4,128,256]{3,2,1,0:T(8,128)(2,1)S(1)}, bf16[2,4,128,256]{3,2,1,0:T(8,128)(2,1)S(1)}, u32[]{:S(2)}, u32[]{:S(2)}) collective-permute-start(bf16[2,4,128,256]{3,2,1,0:T(8,128)(2,1)S(1)} %pad_maximum_fusion.1.x.b0), channel_id=1, source_target_pairs={{0,4},{2,6},{4,0},{6,2},{8,12},{10,14},{12,8},{14,10},{16,20},{18,... | collective-permute-start | bytes 1572872 | tf_op jit(solution)/shard_map/ppermute | solution.py:21
  44.0 11.7 %collective-permute-start.12 = (bf16[2,4,128,256]{3,2,1,0:T(8,128)(2,1)S(1)}, bf16[2,4,128,256]{3,2,1,0:T(8,128)(2,1)S(1)}, u32[]{:S(2)}, u32[]{:S(2)}) collective-permute-start(bf16[2,4,128,256]{3,2,1,0:T(8,128)(2,1)S(1)} %pad_maximum_fusion.1.x.b0), channel_id=1, source_target_pairs={{0,2},{2,0},{4,6},{6,4},{8,10},{10,8},{12,14},{14,12},{16,18},{18,... | collective-permute-start | bytes 1572872 | tf_op jit(solution)/shard_map/ppermute | solution.py:21
  54.4 10.4 %collective-permute-start.15 = (bf16[4,128,256]{2,1,0:T(8,128)(2,1)S(1)}, bf16[4,128,256]{2,1,0:T(8,128)(2,1)S(1)}, u32[]{:S(2)}, u32[]{:S(2)}) collective-permute-start(bf16[4,128,256]{2,1,0:T(8,128)(2,1)S(1)} %slice_bitcast_fusion), channel_id=1, source_target_pairs={{0,2},{2,0},{4,6},{6,4},{8,10},{10,8},{12,14},{14,12},{16,18},{18,... | collective-permute-start | bytes 786440 | tf_op jit(solution)/shard_map/ppermute | solution.py:21
  55.7 9.1 %collective-permute-start.14 = (bf16[4,128,256]{2,1,0:T(8,128)(2,1)S(1)}, bf16[4,128,256]{2,1,0:T(8,128)(2,1)S(1)}, u32[]{:S(2)}, u32[]{:S(2)}) collective-permute-start(bf16[4,128,256]{2,1,0:T(8,128)(2,1)S(1)} %slice_bitcast_fusion.1), channel_id=1, source_target_pairs={{0,4},{2,6},{4,0},{6,2},{8,12},{10,14},{12,8},{14,10},{16,20},{18,... | collective-permute-start | bytes 786440 | tf_op jit(solution)/shard_map/ppermute | solution.py:21
  56.3 8.5 %copy-start.4 = (f32[1,1,2048,256]{3,2,1,0:T(8,128)S(1)}, f32[1,1,2048,256]{3,2,1,0:T(8,128)}, u32[]{:S(2)}) copy-start(f32[1,1,2048,256]{3,2,1,0:T(8,128)} %param.14) | copy-start | bytes 6291460

commit v2 on v1

--- a/solution.py
+++ b/solution.py
@@ -13,7 +13,7 @@
 ANY = pl.ANY
 VMEM = pltpu.VMEM
 SMEM = pltpu.SMEM
-PANEL = 64
+PANEL = 32
 CHUNK = 256
 
 

time: 81.3 us -> 80.8 us (level)
  no operation moved by 1% of the time
where the time goes in v2:
time: 80.8 us; the launch traced here: 80.5 us
  Pallas kernels  42.9 us (53%)
  starting transfers between devices  18.7 us (23%)
  waiting for transfers between devices  9.55 us (12%)
  local copies, waits for them, and re-layouts  5.79 us (7%)
  between operations  1.78 us (2%)
  other arithmetic  1.7 us (2%)
    ppermute x16, starting transfers between devices, exchange(): return lax.ppermute(x, axis, [(r, r ^ bit) for r in range(size)])  18.7 us
    pallas_call x1, Pallas kernels, on_device(): call(functools.partial(second_kernel, masks_a, masks_b, steps), (f32(tile...  15.9 us
    ppermute x16, waiting for transfers between devices, exchange(): return lax.ppermute(x, axis, [(r, r ^ bit) for r in range(size)])  9.55 us
    pallas_call x1, Pallas kernels, on_device(): call(functools.partial(late_kernel, masks_a, steps), (square, square, squ...  8.22 us
    pallas_call x1, Pallas kernels, on_device(): call(functools.partial(cross_kernel, masks_a, steps), f32((1 + steps) * w...  5.53 us
    pallas_call x1, Pallas kernels, on_device(): call(functools.partial(early_kernel, tile), (square, f32(width, 2 * width...  4.79 us
    pallas_call x1, Pallas kernels, on_device(): call(functools.partial(first_kernel, steps), (f32(width, width), f32(widt...  4.55 us
    unnamed x30, local copies, waits for them, and re-layouts  4.02 us
  transfers between devices with their start and end apart: 16, of which 5 were waited for; matrix products, arithmetic and copies ran while one was open for 4% of the time, Pallas kernels for 34%

profile of v2, /device:TPU:0, one launch (start us, length us, event | category | flops | bytes accessed | tf_op | source)
XLA Modules:
  0.0 80.5 jit_solution(1852524665798978645)
XLA Ops:
  0.6 0.5 collective-permute-start.4
  1.2 1.0 %slice_bitcast_fusion.4 = (bf16[1,128,256]{2,1,0:T(8,128)(2,1)S(1)}, bf16[1,128,256]{2,1,0:T(8,128)(2,1)S(1)}, bf16[1,128,256]{2,1,0:T(8,128)(2,1)S(1)}, bf16[1,128,256]{2,1,0:T(8,128)(2,1)S(1)}) fusion(bf16[2,1,128,256]{3,2,1,0:T(8,128)(2,1)} %param.21, bf16[2,1,128,256]{3,2,1,0:T(8,128)(2,1)} %param.20), kind=kLoop, calls=%fused_computation.8 | loop fusion | bytes 524288 | tf_op jit(solution)/shard_map/stack;squeeze | solution.py:526
  2.1 2.7 %collective-permute-start.2 = (bf16[2,1,128,256]{3,2,1,0:T(8,128)(2,1)S(1)}, bf16[2,1,128,256]{3,2,1,0:T(8,128)(2,1)S(1)}, u32[]{:S(2)}, u32[]{:S(2)}) collective-permute-start(bf16[2,1,128,256]{3,2,1,0:T(8,128)(2,1)S(1)} %maximum_bitcast_fusion), channel_id=1, source_target_pairs={{0,8},{2,10},{4,12},{6,14},{8,0},{10,2},{12,4},{14,6},{16,24},{18,... | collective-permute-start | bytes 393224 | tf_op jit(solution)/shard_map/ppermute | solution.py:21
  4.8 2.6 %collective-permute-start.1 = (bf16[2,1,128,256]{3,2,1,0:T(8,128)(2,1)S(1)}, bf16[2,1,128,256]{3,2,1,0:T(8,128)(2,1)}, u32[]{:S(2)}, u32[]{:S(2)}) collective-permute-start(bf16[2,1,128,256]{3,2,1,0:T(8,128)(2,1)S(1)} %maximum_bitcast_fusion), channel_id=1, source_target_pairs={{0,16},{2,18},{4,20},{6,22},{8,24},{10,26},{12,28},{14,30},{16,0},... | collective-permute-start | bytes 393224 | tf_op jit(solution)/shard_map/ppermute | solution.py:21
  7.4 0.0 collective-permute-start
  7.4 1.6 %copy-done = bf16[2,2048,256]{2,1,0:T(8,128)(2,1)S(1)} copy-done((bf16[2,2048,256]{2,1,0:T(8,128)(2,1)S(1)}, bf16[2,2048,256]{2,1,0:T(8,128)(2,1)}, u32[]{:S(2)}) %copy-start) | copy-done | bytes 2097176
  9.0 1.6 %copy-done.3 = f32[1,1,2048,256]{3,2,1,0:T(8,128)S(1)} copy-done((f32[1,1,2048,256]{3,2,1,0:T(8,128)S(1)}, f32[1,1,2048,256]{3,2,1,0:T(8,128)}, u32[]{:S(2)}) %copy-start.3) | copy-done | bytes 2097176
  10.6 0.0 copy-start.12
  10.6 0.0 copy-start.2
  10.6 0.0 copy-start.6
  10.6 1.6 %right_probe.1.refs_5_.core = f32[2,256,256]{2,1,0:T(8,128)S(1)} custom-call(f32[2048,256]{1,0:T(8,128)S(1)} %bitcast.37, bf16[2,2048,256]{2,1,0:T(8,128)(2,1)S(1)} %copy-done), custom_call_target="tpu_custom_call" | custom-call | flops 3221225472 | bytes 1048576 | tf_op jit(solution)/shard_map/right_probe/pallas_call | solution.py:506
  12.2 0.0 copy-start.8
  12.3 0.8 copy-done.8
  13.0 1.2 %collective-permute-done.1 = bf16[2,1,128,256]{3,2,1,0:T(8,128)(2,1)} collective-permute-done((bf16[2,1,128,256]{3,2,1,0:T(8,128)(2,1)S(1)}, bf16[2,1,128,256]{3,2,1,0:T(8,128)(2,1)}, u32[]{:S(2)}, u32[]{:S(2)}) %collective-permute-start.1) | collective-permute-done | bytes 131104 | tf_op jit(solution)/shard_map/ppermute | solution.py:21
  14.3 0.4 collective-permute-start.3
  14.7 0.6 bitcast_multiply_fusion
  16.0 0.7 concatenate.9.scal
  16.7 0.0 collective-permute-done.2
  16.7 2.8 %collective-permute-done.3 = bf16[2,1,128,256]{3,2,1,0:T(8,128)(2,1)} collective-permute-done((bf16[2,1,128,256]{3,2,1,0:T(8,128)(2,1)}, bf16[2,1,128,256]{3,2,1,0:T(8,128)(2,1)}, u32[]{:S(2)}, u32[]{:S(2)}) %collective-permute-start.3) | collective-permute-done | bytes 131104 | tf_op jit(solution)/shard_map/ppermute | solution.py:21
  19.5 1.0 %pad_maximum_fusion.refs_0_.p0 = bf16[2,4,128,256]{3,2,1,0:T(8,128)(2,1)S(1)} fusion(bf16[2,1,128,256]{3,2,1,0:T(8,128)(2,1)} %collective-permute-done.3, bf16[2,1,128,256]{3,2,1,0:T(8,128)(2,1)S(1)} %collective-permute-done.2, bf16[2,1,128,256]{3,2,1,0:T(8,128)(2,1)} %collective-permute-done.1, bf16[2,1,128,256]{3,2,1,0:T(8,128)(2,1)S(1)} %maximum_bitcast_fusion), kind=kLoop, calls=%fused_computation | loop fusion | flops 786432 | bytes 1048576 | tf_op jit(solution)/shard_map/concatenate | solution.py:542
  20.6 0.0 collective-permute-done.4.refs_1_
  20.6 1.6 %collective-permute-start.6 = (bf16[2,4,128,256]{3,2,1,0:T(8,128)(2,1)S(1)}, bf16[2,4,128,256]{3,2,1,0:T(8,128)(2,1)S(1)}, u32[]{:S(2)}, u32[]{:S(2)}) collective-permute-start(bf16[2,4,128,256]{3,2,1,0:T(8,128)(2,1)S(1)} %pad_maximum_fusion.refs_0_.p0), channel_id=1, source_target_pairs={{0,4},{2,6},{4,0},{6,2},{8,12},{10,14},{12,8},{14,10},{16,20},{18,... | collective-permute-start | bytes 1572872 | tf_op jit(solution)/shard_map/ppermute | solution.py:21
  22.2 1.5 %collective-permute-start.5 = (bf16[2,4,128,256]{3,2,1,0:T(8,128)(2,1)S(1)}, bf16[2,4,128,256]{3,2,1,0:T(8,128)(2,1)S(1)}, u32[]{:S(2)}, u32[]{:S(2)}) collective-permute-start(bf16[2,4,128,256]{3,2,1,0:T(8,128)(2,1)S(1)} %pad_maximum_fusion.refs_0_.p0), channel_id=1, source_target_pairs={{0,2},{2,0},{4,6},{6,4},{8,10},{10,8},{12,14},{14,12},{16,18},{18,... | collective-permute-start | bytes 1572872 | tf_op jit(solution)/shard_map/ppermute | solution.py:21
  23.7 1.1 %collective-permute-start.9 = (bf16[2,1,128,256]{3,2,1,0:T(8,128)(2,1)S(1)}, bf16[2,1,128,256]{3,2,1,0:T(8,128)(2,1)S(1)}, u32[]{:S(2)}, u32[]{:S(2)}) collective-permute-start(bf16[2,1,128,256]{3,2,1,0:T(8,128)(2,1)S(1)} %maximum_bitcast_fusion.1), channel_id=1, source_target_pairs={{0,16},{2,18},{4,20},{6,22},{8,24},{10,26},{12,28},{14,30},{16,0},... | collective-permute-start | bytes 393224 | tf_op jit(solution)/shard_map/ppermute | solution.py:21
  24.8 5.5 %left_cross.1.refs_6_.cross = f32[768,768]{1,0:T(8,128)S(1)} custom-call(s32[11]{0:T(128)S(1)} %concatenate.9.scal, f32[2048,256]{1,0:T(8,128)S(1)} %bitcast.35, bf16[1,2,1024,256]{3,2,1,0:T(8,128)(2,1)S(1)} %copy-done.6, bf16[1,2,1024,256]{3,2,1,0:T(8,128)(2,1)} %collective-permute-done.4.refs_1_), custom_call_target="tpu_custom_call" | custom-call | flops 6442450944 | bytes 1048576 | tf_op jit(solution)/shard_map/left_cross/pallas_call | solution.py:515
  30.3 0.0 collective-permute-done.refs_1_
  30.4 2.3 %ordered.1 = (bf16[2048,512]{1,0:T(8,128)(2,1)S(1)}, bf16[2048,512]{1,0:T(8,128)(2,1)S(1)}) custom-call(s32[11]{0:T(128)S(1)} %concatenate.9.scal, bf16[2,2048,256]{2,1,0:T(8,128)(2,1)S(1)} %copy-done.1, bf16[1,2,1024,256]{3,2,1,0:T(8,128)(2,1)S(1)} %copy-done.5, bf16[1,2,1024,256]{3,2,1,0:T(8,128)(2,1)} %collective-permute-done.refs_1_), custom_call_target="tpu_custom_call" | custom-call | flops 1342177280 | bytes 1048576 | tf_op jit(solution)/shard_map/ordered/pallas_call | solution.py:531
  32.7 0.0 copy-start.9
  32.7 0.0 collective-permute-done.6.refs_2_.p2
  32.7 1.1 %collective-permute-done.5.refs_1_.p1 = bf16[2,4,128,256]{3,2,1,0:T(8,128)(2,1)S(1)} collective-permute-done((bf16[2,4,128,256]{3,2,1,0:T(8,128)(2,1)S(1)}, bf16[2,4,128,256]{3,2,1,0:T(8,128)(2,1)S(1)}, u32[]{:S(2)}, u32[]{:S(2)}) %collective-permute-start.5) | collective-permute-done | bytes 524320 | tf_op jit(solution)/shard_map/ppermute | solution.py:21
  33.9 0.6 collective-permute-start.7
  34.5 1.5 %collective-permute-start.8 = (bf16[4,128,256]{2,1,0:T(8,128)(2,1)S(1)}, bf16[4,128,256]{2,1,0:T(8,128)(2,1)S(1)}, u32[]{:S(2)}, u32[]{:S(2)}) collective-permute-start(bf16[4,128,256]{2,1,0:T(8,128)(2,1)S(1)} %slice_bitcast_fusion.2), channel_id=1, source_target_pairs={{0,2},{2,0},{4,6},{6,4},{8,10},{10,8},{12,14},{14,12},{16,18},{18,... | collective-permute-start | bytes 786440 | tf_op jit(solution)/shard_map/ppermute | solution.py:21
  36.0 1.1 %collective-permute-start.10 = (bf16[2,1,128,256]{3,2,1,0:T(8,128)(2,1)S(1)}, bf16[2,1,128,256]{3,2,1,0:T(8,128)(2,1)S(1)}, u32[]{:S(2)}, u32[]{:S(2)}) collective-permute-start(bf16[2,1,128,256]{3,2,1,0:T(8,128)(2,1)S(1)} %maximum_bitcast_fusion.1), channel_id=1, source_target_pairs={{0,8},{2,10},{4,12},{6,14},{8,0},{10,2},{12,4},{14,6},{16,24},{18,... | collective-permute-start | bytes 393224 | tf_op jit(solution)/shard_map/ppermute | solution.py:21
  37.1 0.0 collective-permute-done.9
  37.1 0.9 %collective-permute-start.11 = (bf16[2,1,128,256]{3,2,1,0:T(8,128)(2,1)S(1)}, bf16[2,1,128,256]{3,2,1,0:T(8,128)(2,1)S(1)}, u32[]{:S(2)}, u32[]{:S(2)}) collective-permute-start(bf16[2,1,128,256]{3,2,1,0:T(8,128)(2,1)S(1)} %collective-permute-done.9), channel_id=1, source_target_pairs={{0,8},{2,10},{4,12},{6,14},{8,0},{10,2},{12,4},{14,6},{16,24},{18,... | collective-permute-start | bytes 393224 | tf_op jit(solution)/shard_map/ppermute | solution.py:21
  38.0 2.9 %collective-permute-done.10 = bf16[2,1,128,256]{3,2,1,0:T(8,128)(2,1)S(1)} collective-permute-done((bf16[2,1,128,256]{3,2,1,0:T(8,128)(2,1)S(1)}, bf16[2,1,128,256]{3,2,1,0:T(8,128)(2,1)S(1)}, u32[]{:S(2)}, u32[]{:S(2)}) %collective-permute-start.10) | collective-permute-done | bytes 131104 | tf_op jit(solution)/shard_map/ppermute | solution.py:21
  40.9 1.4 %collective-permute-done.11 = bf16[2,1,128,256]{3,2,1,0:T(8,128)(2,1)S(1)} collective-permute-done((bf16[2,1,128,256]{3,2,1,0:T(8,128)(2,1)S(1)}, bf16[2,1,128,256]{3,2,1,0:T(8,128)(2,1)S(1)}, u32[]{:S(2)}, u32[]{:S(2)}) %collective-permute-start.11) | collective-permute-done | bytes 131104 | tf_op jit(solution)/shard_map/ppermute | solution.py:21
  42.3 0.1 pad_maximum_fusion.1.x.b0
  42.4 0.0 collective-permute-done.8.refs_4_.pr3
  42.4 1.6 %collective-permute-start.13 = (bf16[2,4,128,256]{3,2,1,0:T(8,128)(2,1)S(1)}, bf16[2,4,128,256]{3,2,1,0:T(8,128)(2,1)S(1)}, u32[]{:S(2)}, u32[]{:S(2)}) collective-permute-start(bf16[2,4,128,256]{3,2,1,0:T(8,128)(2,1)S(1)} %pad_maximum_fusion.1.x.b0), channel_id=1, source_target_pairs={{0,4},{2,6},{4,0},{6,2},{8,12},{10,14},{12,8},{14,10},{16,20},{18,... | collective-permute-start | bytes 1572872 | tf_op jit(solution)/shard_map/ppermute | solution.py:21
  44.0 0.8 collective-permute-start.12
  44.8 4.5 %first_step.1 = (f32[256,256]{1,0:T(8,128)S(1)}, f32[256,256]{1,0:T(8,128)S(1)}, f32[512,256]{1,0:T(8,128)S(1)}, f32[512,256]{1,0:T(8,128)S(1)}, f32[256,256]{1,0:T(8,128)S(1)}) custom-call(s32[11]{0:T(128)S(1)} %concatenate.9.scal, bf16[2048,512]{1,0:T(8,128)(2,1)S(1)} %get-tuple-element.26.ar, bf16[2048,512]{1,0:T(8,128)(2,1)S(1)} %get-tuple-element.27.probe, ...), custom_call_target="tpu_custom_call" | custom-call | flops 5368709120 | bytes 1048576 | tf_op jit(solution)/shard_map/first_step/pallas_call | solution.py:554
  49.4 4.8 %factor_early.1 = (f32[256,256]{1,0:T(8,128)S(1)}, f32[256,512]{1,0:T(8,128)S(1)}) custom-call(s32[11]{0:T(128)S(1)} %concatenate.9.scal, f32[256,256]{1,0:T(8,128)S(1)} %get-tuple-element.31.gram, f32[512,256]{1,0:T(8,128)S(1)} %get-tuple-element.32.k0, f32[512,256]{1,0:T(8,128)S(1)} %get-tuple-element.33.y0, f32[768,768]{1,0:T(8,128)S(1)} %left_cross.1.refs_6_.cross, ...), custom_call_target="tpu_custom_call" | custom-call | flops 4026531840 | bytes 1048576 | tf_op jit(solution)/shard_map/factor_early/pallas_call | solution.py:564
  54.2 1.3 %collective-permute-start.15 = (bf16[4,128,256]{2,1,0:T(8,128)(2,1)S(1)}, bf16[4,128,256]{2,1,0:T(8,128)(2,1)S(1)}, u32[]{:S(2)}, u32[]{:S(2)}) collective-permute-start(bf16[4,128,256]{2,1,0:T(8,128)(2,1)S(1)} %slice_bitcast_fusion), channel_id=1, source_target_pairs={{0,2},{2,0},{4,6},{6,4},{8,10},{10,8},{12,14},{14,12},{16,18},{18,... | collective-permute-start | bytes 786440 | tf_op jit(solution)/shard_map/ppermute | solution.py:21
  55.5 0.6 collective-permute-start.14
  56.1 8.2 %factor_late.1 = (f32[256,256]{1,0:T(8,128)S(1)}, f32[256,256]{1,0:T(8,128)S(1)}, f32[256,256]{1,0:T(8,128)S(1)}, f32[256,256]{1,0:T(8,128)S(1)}, f32[256,256]{1...) custom-call(s32[11]{0:T(128)S(1)} %concatenate.9.scal, ...), custom_call_target="tpu_custom_call" | custom-call | flops 6710886400 | bytes 1048576 | tf_op jit(solution)/shard_map/factor_late/pallas_call | solution.py:575
  64.3 0.0 collective-permute-done.15.r3.br3
  64.4 15.9 %second_step.1 = (f32[2048,256]{1,0:T(8,128)}, f32[2048,256]{1,0:T(8,128)}) custom-call(s32[11]{0:T(128)S(1)} %concatenate.9.scal, f32[256,256]{1,0:T(8,128)S(1)} %get-tuple-element.40.core_c, f32[256,256]{1,0:T(8,128)S(1)} %get-tuple-element.41.h0, f32[256,256]{1,0:T(8,128)S(1)} %get-tuple-element.42.h_a, f32[256,256]{1,0:T(8,128)S(1)} %get-tuple-element.43.mid_part, ...), custom_call_target="tpu_custom_call" | custom-call | flops 26843545600 | bytes 1048576 | tf_op jit(solution)/shard_map/second_step/pallas_call | solution.py:584
  (32 shorter events, 0.2 us)
Async XLA Ops:
  0.6 20.0 %collective-permute-start.4 = (bf16[1,2,1024,256]{3,2,1,0:T(8,128)(2,1)}, bf16[1,2,1024,256]{3,2,1,0:T(8,128)(2,1)}, u32[]{:S(2)}, u32[]{:S(2)}) collective-permute-start(bf16[1,2,1024,256]{3,2,1,0:T(8,128)(2,1)} %refs_0_.7), channel_id=1, source_target_pairs={{0,1},{1,0},{2,3},{3,2},{4,5},{5,4},{6,7},{7,6},{8,9},{9,8},{10,11... | collective-permute-start | bytes 3145736 | tf_op jit(solution)/shard_map/ppermute | solution.py:21
  2.1 14.6 %collective-permute-start.2 = (bf16[2,1,128,256]{3,2,1,0:T(8,128)(2,1)S(1)}, bf16[2,1,128,256]{3,2,1,0:T(8,128)(2,1)S(1)}, u32[]{:S(2)}, u32[]{:S(2)}) collective-permute-start(bf16[2,1,128,256]{3,2,1,0:T(8,128)(2,1)S(1)} %maximum_bitcast_fusion), channel_id=1, source_target_pairs={{0,8},{2,10},{4,12},{6,14},{8,0},{10,2},{12,4},{14,6},{16,24},{18,... | collective-permute-start | bytes 393224 | tf_op jit(solution)/shard_map/ppermute | solution.py:21
  4.8 9.5 %collective-permute-start.1 = (bf16[2,1,128,256]{3,2,1,0:T(8,128)(2,1)S(1)}, bf16[2,1,128,256]{3,2,1,0:T(8,128)(2,1)}, u32[]{:S(2)}, u32[]{:S(2)}) collective-permute-start(bf16[2,1,128,256]{3,2,1,0:T(8,128)(2,1)S(1)} %maximum_bitcast_fusion), channel_id=1, source_target_pairs={{0,16},{2,18},{4,20},{6,22},{8,24},{10,26},{12,28},{14,30},{16,0},... | collective-permute-start | bytes 393224 | tf_op jit(solution)/shard_map/ppermute | solution.py:21
  7.4 23.0 %collective-permute-start = (bf16[1,2,1024,256]{3,2,1,0:T(8,128)(2,1)}, bf16[1,2,1024,256]{3,2,1,0:T(8,128)(2,1)}, u32[]{:S(2)}, u32[]{:S(2)}) collective-permute-start(bf16[1,2,1024,256]{3,2,1,0:T(8,128)(2,1)} %refs_0_.4), channel_id=1, source_target_pairs={{0,1},{1,0},{2,3},{3,2},{4,5},{5,4},{6,7},{7,6},{8,9},{9,8},{10,11... | collective-permute-start | bytes 3145736 | tf_op jit(solution)/shard_map/ppermute | solution.py:21
  7.4 1.6 %copy-start = (bf16[2,2048,256]{2,1,0:T(8,128)(2,1)S(1)}, bf16[2,2048,256]{2,1,0:T(8,128)(2,1)}, u32[]{:S(2)}) copy-start(bf16[2,2048,256]{2,1,0:T(8,128)(2,1)} %probe.3) | copy-start | bytes 6291460
  9.0 1.6 %copy-start.3 = (f32[1,1,2048,256]{3,2,1,0:T(8,128)S(1)}, f32[1,1,2048,256]{3,2,1,0:T(8,128)}, u32[]{:S(2)}) copy-start(f32[1,1,2048,256]{3,2,1,0:T(8,128)} %param.14) | copy-start | bytes 6291460
  10.6 4.1 %copy-start.13 = (s32[2,1]{0,1:T(1,128)S(1)}, s32[2,1]{0,1:T(1,128)}, u32[]{:S(2)}) copy-start(s32[2,1]{0,1:T(1,128)} %param.23) | copy-start | bytes 28
  10.6 4.1 %copy-start.14 = (s32[1,2]{1,0:T(1,128)S(1)}, s32[1,2]{1,0:T(1,128)}, u32[]{:S(2)}) copy-start(s32[1,2]{1,0:T(1,128)} %param.19) | copy-start | bytes 28
  10.6 5.4 %copy-start.10 = (s32[1,1,2]{2,1,0:T(1,128)S(1)}, s32[1,1,2]{2,1,0:T(1,128)}, u32[]{:S(2)}) copy-start(s32[1,1,2]{2,1,0:T(1,128)} %param.25) | copy-start | bytes 28
  10.6 5.4 %copy-start.11 = (s32[1,2]{1,0:T(1,128)S(1)}, s32[1,2]{1,0:T(1,128)}, u32[]{:S(2)}) copy-start(s32[1,2]{1,0:T(1,128)} %param.18) | copy-start | bytes 28
  10.6 5.4 %copy-start.12 = (s32[2,1]{0,1:T(1,128)S(1)}, s32[2,1]{0,1:T(1,128)}, u32[]{:S(2)}) copy-start(s32[2,1]{0,1:T(1,128)} %param.22) | copy-start | bytes 28
  10.6 14.2 %copy-start.2 = (f32[1,1,2048,256]{3,2,1,0:T(8,128)S(1)}, f32[1,1,2048,256]{3,2,1,0:T(8,128)}, u32[]{:S(2)}) copy-start(f32[1,1,2048,256]{3,2,1,0:T(8,128)} %param.13) | copy-start | bytes 6291460
  10.6 14.2 %copy-start.6 = (bf16[1,2,1024,256]{3,2,1,0:T(8,128)(2,1)S(1)}, bf16[1,2,1024,256]{3,2,1,0:T(8,128)(2,1)}, u32[]{:S(2)}) copy-start(bf16[1,2,1024,256]{3,2,1,0:T(8,128)(2,1)} %refs_0_.7) | copy-start | bytes 3145732
  12.2 0.8 copy-start.8
  14.3 5.3 %collective-permute-start.3 = (bf16[2,1,128,256]{3,2,1,0:T(8,128)(2,1)}, bf16[2,1,128,256]{3,2,1,0:T(8,128)(2,1)}, u32[]{:S(2)}, u32[]{:S(2)}) collective-permute-start(bf16[2,1,128,256]{3,2,1,0:T(8,128)(2,1)} %collective-permute-done.1), channel_id=1, source_target_pairs={{0,8},{2,10},{4,12},{6,14},{8,0},{10,2},{12,4},{14,6},{16,24},{18,... | collective-permute-start | bytes 393224 | tf_op jit(solution)/shard_map/ppermute | solution.py:21
  20.6 12.1 %collective-permute-start.6 = (bf16[2,4,128,256]{3,2,1,0:T(8,128)(2,1)S(1)}, bf16[2,4,128,256]{3,2,1,0:T(8,128)(2,1)S(1)}, u32[]{:S(2)}, u32[]{:S(2)}) collective-permute-start(bf16[2,4,128,256]{3,2,1,0:T(8,128)(2,1)S(1)} %pad_maximum_fusion.refs_0_.p0), channel_id=1, source_target_pairs={{0,4},{2,6},{4,0},{6,2},{8,12},{10,14},{12,8},{14,10},{16,20},{18,... | collective-permute-start | bytes 1572872 | tf_op jit(solution)/shard_map/ppermute | solution.py:21
  22.2 11.7 %collective-permute-start.5 = (bf16[2,4,128,256]{3,2,1,0:T(8,128)(2,1)S(1)}, bf16[2,4,128,256]{3,2,1,0:T(8,128)(2,1)S(1)}, u32[]{:S(2)}, u32[]{:S(2)}) collective-permute-start(bf16[2,4,128,256]{3,2,1,0:T(8,128)(2,1)S(1)} %pad_maximum_fusion.refs_0_.p0), channel_id=1, source_target_pairs={{0,2},{2,0},{4,6},{6,4},{8,10},{10,8},{12,14},{14,12},{16,18},{18,... | collective-permute-start | bytes 1572872 | tf_op jit(solution)/shard_map/ppermute | solution.py:21
  23.7 13.4 %collective-permute-start.9 = (bf16[2,1,128,256]{3,2,1,0:T(8,128)(2,1)S(1)}, bf16[2,1,128,256]{3,2,1,0:T(8,128)(2,1)S(1)}, u32[]{:S(2)}, u32[]{:S(2)}) collective-permute-start(bf16[2,1,128,256]{3,2,1,0:T(8,128)(2,1)S(1)} %maximum_bitcast_fusion.1), channel_id=1, source_target_pairs={{0,16},{2,18},{4,20},{6,22},{8,24},{10,26},{12,28},{14,30},{16,0},... | collective-permute-start | bytes 393224 | tf_op jit(solution)/shard_map/ppermute | solution.py:21
  24.8 5.6 %copy-start.1 = (bf16[2,2048,256]{2,1,0:T(8,128)(2,1)S(1)}, bf16[2,2048,256]{2,1,0:T(8,128)(2,1)}, u32[]{:S(2)}) copy-start(bf16[2,2048,256]{2,1,0:T(8,128)(2,1)} %probe.3) | copy-start | bytes 6291460
  24.8 5.6 %copy-start.5 = (bf16[1,2,1024,256]{3,2,1,0:T(8,128)(2,1)S(1)}, bf16[1,2,1024,256]{3,2,1,0:T(8,128)(2,1)}, u32[]{:S(2)}) copy-start(bf16[1,2,1024,256]{3,2,1,0:T(8,128)(2,1)} %refs_0_.4) | copy-start | bytes 3145732
  30.3 19.0 %copy-start.7 = (f32[768,768]{1,0:T(8,128)}, f32[768,768]{1,0:T(8,128)S(1)}, u32[]{:S(2)}) copy-start(f32[768,768]{1,0:T(8,128)S(1)} %left_cross.1.refs_6_.cross) | copy-start | bytes 7077892
  32.7 12.1 %copy-start.9 = (f32[2,256,256]{2,1,0:T(8,128)S(1)}, f32[2,256,256]{2,1,0:T(8,128)}, u32[]{:S(2)}) copy-start(f32[2,256,256]{2,1,0:T(8,128)} %copy-done.8) | copy-start | bytes 1572868
  33.9 8.5 %collective-permute-start.7 = (bf16[4,128,256]{2,1,0:T(8,128)(2,1)S(1)}, bf16[4,128,256]{2,1,0:T(8,128)(2,1)S(1)}, u32[]{:S(2)}, u32[]{:S(2)}) collective-permute-start(bf16[4,128,256]{2,1,0:T(8,128)(2,1)S(1)} %slice_bitcast_fusion.3), channel_id=1, source_target_pairs={{0,4},{2,6},{4,0},{6,2},{8,12},{10,14},{12,8},{14,10},{16,20},{18,... | collective-permute-start | bytes 786440 | tf_op jit(solution)/shard_map/ppermute | solution.py:21
  34.5 7.9 %collective-permute-start.8 = (bf16[4,128,256]{2,1,0:T(8,128)(2,1)S(1)}, bf16[4,128,256]{2,1,0:T(8,128)(2,1)S(1)}, u32[]{:S(2)}, u32[]{:S(2)}) collective-permute-start(bf16[4,128,256]{2,1,0:T(8,128)(2,1)S(1)} %slice_bitcast_fusion.2), channel_id=1, source_target_pairs={{0,2},{2,0},{4,6},{6,4},{8,10},{10,8},{12,14},{14,12},{16,18},{18,... | collective-permute-start | bytes 786440 | tf_op jit(solution)/shard_map/ppermute | solution.py:21
  36.0 5.0 %collective-permute-start.10 = (bf16[2,1,128,256]{3,2,1,0:T(8,128)(2,1)S(1)}, bf16[2,1,128,256]{3,2,1,0:T(8,128)(2,1)S(1)}, u32[]{:S(2)}, u32[]{:S(2)}) collective-permute-start(bf16[2,1,128,256]{3,2,1,0:T(8,128)(2,1)S(1)} %maximum_bitcast_fusion.1), channel_id=1, source_target_pairs={{0,8},{2,10},{4,12},{6,14},{8,0},{10,2},{12,4},{14,6},{16,24},{18,... | collective-permute-start | bytes 393224 | tf_op jit(solution)/shard_map/ppermute | solution.py:21
  37.1 5.2 %collective-permute-start.11 = (bf16[2,1,128,256]{3,2,1,0:T(8,128)(2,1)S(1)}, bf16[2,1,128,256]{3,2,1,0:T(8,128)(2,1)S(1)}, u32[]{:S(2)}, u32[]{:S(2)}) collective-permute-start(bf16[2,1,128,256]{3,2,1,0:T(8,128)(2,1)S(1)} %collective-permute-done.9), channel_id=1, source_target_pairs={{0,8},{2,10},{4,12},{6,14},{8,0},{10,2},{12,4},{14,6},{16,24},{18,... | collective-permute-start | bytes 393224 | tf_op jit(solution)/shard_map/ppermute | solution.py:21
  42.4 11.8 %collective-permute-start.13 = (bf16[2,4,128,256]{3,2,1,0:T(8,128)(2,1)S(1)}, bf16[2,4,128,256]{3,2,1,0:T(8,128)(2,1)S(1)}, u32[]{:S(2)}, u32[]{:S(2)}) collective-permute-start(bf16[2,4,128,256]{3,2,1,0:T(8,128)(2,1)S(1)} %pad_maximum_fusion.1.x.b0), channel_id=1, source_target_pairs={{0,4},{2,6},{4,0},{6,2},{8,12},{10,14},{12,8},{14,10},{16,20},{18,... | collective-permute-start | bytes 1572872 | tf_op jit(solution)/shard_map/ppermute | solution.py:21
  44.0 11.5 %collective-permute-start.12 = (bf16[2,4,128,256]{3,2,1,0:T(8,128)(2,1)S(1)}, bf16[2,4,128,256]{3,2,1,0:T(8,128)(2,1)S(1)}, u32[]{:S(2)}, u32[]{:S(2)}) collective-permute-start(bf16[2,4,128,256]{3,2,1,0:T(8,128)(2,1)S(1)} %pad_maximum_fusion.1.x.b0), channel_id=1, source_target_pairs={{0,2},{2,0},{4,6},{6,4},{8,10},{10,8},{12,14},{14,12},{16,18},{18,... | collective-permute-start | bytes 1572872 | tf_op jit(solution)/shard_map/ppermute | solution.py:21
  54.2 10.1 %collective-permute-start.15 = (bf16[4,128,256]{2,1,0:T(8,128)(2,1)S(1)}, bf16[4,128,256]{2,1,0:T(8,128)(2,1)S(1)}, u32[]{:S(2)}, u32[]{:S(2)}) collective-permute-start(bf16[4,128,256]{2,1,0:T(8,128)(2,1)S(1)} %slice_bitcast_fusion), channel_id=1, source_target_pairs={{0,2},{2,0},{4,6},{6,4},{8,10},{10,8},{12,14},{14,12},{16,18},{18,... | collective-permute-start | bytes 786440 | tf_op jit(solution)/shard_map/ppermute | solution.py:21
  55.5 8.8 %collective-permute-start.14 = (bf16[4,128,256]{2,1,0:T(8,128)(2,1)S(1)}, bf16[4,128,256]{2,1,0:T(8,128)(2,1)S(1)}, u32[]{:S(2)}, u32[]{:S(2)}) collective-permute-start(bf16[4,128,256]{2,1,0:T(8,128)(2,1)S(1)} %slice_bitcast_fusion.1), channel_id=1, source_target_pairs={{0,4},{2,6},{4,0},{6,2},{8,12},{10,14},{12,8},{14,10},{16,20},{18,... | collective-permute-start | bytes 786440 | tf_op jit(solution)/shard_map/ppermute | solution.py:21
  56.1 8.2 %copy-start.4 = (f32[1,1,2048,256]{3,2,1,0:T(8,128)S(1)}, f32[1,1,2048,256]{3,2,1,0:T(8,128)}, u32[]{:S(2)}) copy-start(f32[1,1,2048,256]{3,2,1,0:T(8,128)} %param.14) | copy-start | bytes 6291460
